TPU v7x, 768 devices: a whole 4x8x12 slice. The times are simulated.
768 devices in a mesh: path: 48 (over z, y_lo), shard: 16 (over y_hi, x, core).
Axes of the slice: x: 4, y: 8 (y_hi: 2, y_lo: 4; y = y_hi * 4 + y_lo), z: 12, core: 2. Of those that a mesh axis runs over, the one named last changes fastest.
Arguments:
- tokens: bfloat16 [9216, 2112], P('path'), may hold values from -6 to 6
- out_grad: bfloat16 [9216, 2112], P('path'), may hold values from -0.059814453 to 0.059814453
- doc_lengths: int32 [48, 24], P('path'), may hold values from 1 to 16, 192 in all within a row
- doc_paths: int32 [48, 24], P('path'), may hold values from 0 to 47
- membership: int32 [48, 2], replicated, may hold values from 0 to 3
- up_master: float32 [4, 2112, 8192], P(None, 'path', 'shard'), may hold values from -0.9574271 to 0.9574271
- down_master: float32 [4, 2112, 8192], P(None, 'path', 'shard'), may hold values from -0.4861359 to 0.4861359
- up_moment: bfloat16 [4, 2112, 8192], P(None, 'path', 'shard'), may hold values from -0.059814453 to 0.059814453
- down_moment: bfloat16 [4, 2112, 8192], P(None, 'path', 'shard'), may hold values from -0.059814453 to 0.059814453
Outputs:
- new_up_master: float32 [4, 2112, 8192], P(None, 'path', 'shard')
- new_down_master: float32 [4, 2112, 8192], P(None, 'path', 'shard')
- new_up_moment: bfloat16 [4, 2112, 8192], P(None, 'path', 'shard')
- new_down_moment: bfloat16 [4, 2112, 8192], P(None, 'path', 'shard')
All inputs are finite; a program needn't handle non-finite values.
Results may differ from a plain program's by a relative error of at most 0.005.
The roundings to bfloat16 on the way count: a program that leaves them out, or rounds other values in their place, can miss the bound.
Values may be sent and summed in bfloat16 or wider, within the bound.
A program may use at most 64 MiB of HBM per device.

v0:
```python
import jax
import jax.numpy as jnp
from jax import lax
from jax.sharding import PartitionSpec as P

FF = 8192


norm_epsilon = 1e-06
hidden_epsilon = 1e-05
adam_epsilon = 0.001
inner_rate = 0.05
decay_rate = 0.1
outer_rate = 0.7
momentum_coef = 0.9
gelu_coef = 0.7978845608
cubic_coef = 0.044715


def gelu_pair(values):
    inner = gelu_coef * (values + cubic_coef * values * values * values)
    tangent = jnp.tanh(inner)
    activated = 0.5 * values * (1.0 + tangent)
    slopes = 0.5 * (1.0 + tangent) + 0.5 * values * (1.0 - tangent * tangent) * gelu_coef * (
        1.0 + 3.0 * cubic_coef * values * values
    )
    return (activated, slopes)


def placing_matrix(lengths, targets, row_count, path_count, capacity):
    ends = jnp.cumsum(lengths)
    row_ids = jnp.arange(row_count, dtype=jnp.int32)
    doc_of_row = jnp.sum((row_ids[:, None] >= ends[None, :]).astype(jnp.int32), axis=1)
    doc_hit = doc_of_row[:, None] == jnp.arange(lengths.shape[0], dtype=jnp.int32)[None, :]
    row_path = jnp.sum(jnp.where(doc_hit, targets[None, :], 0), axis=1)
    path_hit = (row_path[:, None] == jnp.arange(path_count, dtype=jnp.int32)[None, :]).astype(
        jnp.int32
    )
    ranks = jnp.sum((jnp.cumsum(path_hit, axis=0) - 1) * path_hit, axis=1)
    slots = jnp.where(ranks < capacity, row_path * capacity + ranks, -1)
    return (jnp.arange(path_count * capacity, dtype=jnp.int32)[:, None] == slots[None, :]).astype(
        jnp.bfloat16
    )


def adam_delta(gradient, weight):
    update = gradient / (jnp.abs(gradient) + adam_epsilon) + decay_rate * weight.astype(jnp.float32)
    return (-inner_rate * update).astype(jnp.bfloat16)


def outer_update(master, moment, summed, counts):
    pseudo = -summed / jnp.maximum(counts, 1.0)[:, None, None]
    buffer = momentum_coef * moment.astype(jnp.float32) + pseudo
    return (master - outer_rate * (pseudo + momentum_coef * buffer), buffer.astype(jnp.bfloat16))


def on_device(
    tokens,
    out_grad,
    doc_lengths,
    doc_paths,
    membership,
    up_master,
    down_master,
    up_moment,
    down_moment,
):
    path_count = lax.axis_size("path")
    row_count = tokens.shape[0]
    module_count = up_master.shape[0]
    owner_rows = up_master.shape[1]
    half_width = up_master.shape[2] // 2
    capacity = row_count // path_count
    placing = placing_matrix(doc_lengths[0], doc_paths[0], row_count, path_count, capacity)
    sent_rows = jnp.dot(placing, tokens, preferred_element_type=jnp.float32).astype(jnp.bfloat16)
    sent_grads = jnp.dot(placing, out_grad, preferred_element_type=jnp.float32).astype(jnp.bfloat16)
    rows_in, grads_in = (
        lax.all_to_all(sent_rows, "path", split_axis=0, concat_axis=0, tiled=True),
        lax.all_to_all(sent_grads, "path", split_axis=0, concat_axis=0, tiled=True),
    )
    masters = (up_master, down_master)
    moments = (up_moment, down_moment)

    def fetch(which_level):
        table_column = membership[:, which_level]
        halves = []
        for half_index in range(2):
            piece = masters[which_level][
                :, :, half_index * half_width : (half_index + 1) * half_width
            ].astype(jnp.bfloat16)
            outgoing = jnp.take(piece, table_column, axis=0)
            incoming = lax.all_to_all(outgoing, "path", split_axis=0, concat_axis=1, tiled=True)
            halves.append(incoming[0])
        return jnp.concatenate(halves, axis=1)

    def ship(which_level, gradient, weight):
        delta = adam_delta(gradient, weight)
        table_column = membership[:, which_level]
        selector = jnp.arange(module_count, dtype=jnp.int32)[:, None] == table_column[None, :]
        counts = jnp.sum(selector.astype(jnp.float32), axis=1)
        selector_b = selector.astype(jnp.bfloat16)
        summed_halves = []
        for half_index in range(2):
            outgoing = delta[:, half_index * half_width : (half_index + 1) * half_width].reshape(
                path_count, owner_rows, half_width
            )
            incoming = lax.all_to_all(outgoing, "path", split_axis=0, concat_axis=0, tiled=True)
            summed = jnp.dot(
                selector_b,
                incoming.reshape(path_count, owner_rows * half_width),
                preferred_element_type=jnp.float32,
            )
            summed_halves.append(summed.reshape(module_count, owner_rows, half_width))
        summed_all = jnp.concatenate(summed_halves, axis=2)
        return outer_update(masters[which_level], moments[which_level], summed_all, counts)

    up_weight = fetch(0)
    down_weight = fetch(1)
    rows_float = rows_in.astype(jnp.float32)
    normed = (
        rows_float
        * lax.rsqrt(jnp.mean(rows_float * rows_float, axis=1, keepdims=True) + norm_epsilon)
    ).astype(jnp.bfloat16)
    pre = jnp.dot(normed, up_weight, preferred_element_type=jnp.float32)
    activated, slopes = gelu_pair(pre)
    squares = lax.psum(jnp.sum(activated * activated, axis=1), "shard")
    scale = jnp.sqrt(squares / FF + hidden_epsilon)[:, None]
    hidden = activated / scale
    hidden_b = hidden.astype(jnp.bfloat16)
    grad_down = jnp.dot(grads_in.T, hidden_b, preferred_element_type=jnp.float32)
    back = jnp.dot(grads_in, down_weight, preferred_element_type=jnp.float32)
    products = lax.psum(jnp.sum(back * hidden, axis=1), "shard")
    mixing = (products / FF)[:, None]
    dpre = ((back - hidden * mixing) / scale * slopes).astype(jnp.bfloat16)
    grad_up = jnp.dot(normed.T, dpre, preferred_element_type=jnp.float32)
    up_result = ship(0, grad_up, up_weight)
    down_result = ship(1, grad_down, down_weight)
    return (up_result[0], down_result[0], up_result[1], down_result[1])


def solution(mesh):
    return jax.shard_map(
        on_device,
        mesh=mesh,
        in_specs=(
            P("path", None),
            P("path", None),
            P("path", None),
            P("path", None),
            P(),
            P(None, "path", "shard"),
            P(None, "path", "shard"),
            P(None, "path", "shard"),
            P(None, "path", "shard"),
        ),
        out_specs=(
            P(None, "path", "shard"),
            P(None, "path", "shard"),
            P(None, "path", "shard"),
            P(None, "path", "shard"),
        ),
        check_vma=False,
    )
```

profile of v0, /device:TPU:56, one launch (start us, length us, event | category | flops | bytes accessed | tf_op | source)
XLA Modules:
  0.0 559.4 jit_solution(4403184949803949909)
XLA Ops:
  5.0 18.9 %all-to-all-start.1 = ((bf16[48,4,2112]{2,1,0:T(4,128)(2,1)}), bf16[48,4,2112]{2,1,0:T(4,128)(2,1)S(1)}, u32[]{:S(2)}, u32[]{:S(2)}) async-start(bf16[48,4,2112]{2,1,0:T(4,128)(2,1)} %all_to_all.56), calls=%async_computation.1 | async-start | bytes 1671168 | tf_op jit(solution)/shard_map/all_to_all | solution.py:79
  25.4 29.7 %all-to-all-done.1 = bf16[48,4,2112]{2,1,0:T(4,128)(2,1)S(1)} async-done(((bf16[48,4,2112]{2,1,0:T(4,128)(2,1)}), bf16[48,4,2112]{2,1,0:T(4,128)(2,1)S(1)}, u32[]{:S(2)}, u32[]{:S(2)}) %all-to-all-start.1) | async-done | bytes 811040 | tf_op jit(solution)/shard_map/all_to_all | solution.py:79
  56.0 9.7 %all-to-all-start = ((bf16[48,4,2112]{2,1,0:T(4,128)(2,1)}), bf16[48,4,2112]{2,1,0:T(4,128)(2,1)S(1)}, u32[]{:S(2)}, u32[]{:S(2)}) async-start(bf16[48,4,2112]{2,1,0:T(4,128)(2,1)} %all_to_all.54), calls=%async_computation | async-start | bytes 1671168 | tf_op jit(solution)/shard_map/all_to_all | solution.py:78
  68.3 3.0 broadcast_select_fusion.2
  71.3 25.2 %all-to-all-done = bf16[48,4,2112]{2,1,0:T(4,128)(2,1)S(1)} async-done(((bf16[48,4,2112]{2,1,0:T(4,128)(2,1)}), bf16[48,4,2112]{2,1,0:T(4,128)(2,1)S(1)}, u32[]{:S(2)}, u32[]{:S(2)}) %all-to-all-start) | async-done | bytes 811040 | tf_op jit(solution)/shard_map/all_to_all | solution.py:78
  96.5 9.9 %all-to-all-start.2 = ((bf16[48,44,256]{2,1,0:T(8,128)(2,1)}), bf16[48,44,256]{2,1,0:T(8,128)(2,1)}, u32[]{:S(2)}, u32[]{:S(2)}) async-start(bf16[48,44,256]{2,1,0:T(8,128)(2,1)} %get-tuple-element.26), calls=%async_computation.2 | async-start | bytes 2359296 | tf_op jit(solution)/shard_map/all_to_all | solution.py:92
  109.0 3.0 broadcast_select_fusion
  111.9 36.0 %all-to-all-done.2 = bf16[48,44,256]{2,1,0:T(8,128)(2,1)} async-done(((bf16[48,44,256]{2,1,0:T(8,128)(2,1)}), bf16[48,44,256]{2,1,0:T(8,128)(2,1)}, u32[]{:S(2)}, u32[]{:S(2)}) %all-to-all-start.2) | async-done | bytes 1081376 | tf_op jit(solution)/shard_map/all_to_all | solution.py:92
  148.0 51.3 %all_to_all.77 = bf16[48,44,256]{2,1,0:T(8,128)(2,1)} all-to-all(bf16[48,44,256]{2,1,0:T(8,128)(2,1)} %get-tuple-element.27), channel_id=1, replica_groups=mesh['path'=48,'shard'=16] {'path'}, dimensions={0} | all-to-all | bytes 2162688 | tf_op jit(solution)/shard_map/all_to_all | solution.py:92
  199.3 51.3 %all_to_all.78 = bf16[48,44,256]{2,1,0:T(8,128)(2,1)} all-to-all(bf16[48,44,256]{2,1,0:T(8,128)(2,1)S(1)} %copy-done.2), channel_id=1, replica_groups=mesh['path'=48,'shard'=16] {'path'}, dimensions={0} | all-to-all | bytes 2162688 | tf_op jit(solution)/shard_map/all_to_all | solution.py:92
  250.6 10.2 %all-to-all-start.3 = ((bf16[48,44,256]{2,1,0:T(8,128)(2,1)}), bf16[48,44,256]{2,1,0:T(8,128)(2,1)}, u32[]{:S(2)}, u32[]{:S(2)}) async-start(bf16[48,44,256]{2,1,0:T(8,128)(2,1)} %get-tuple-element.25), calls=%async_computation.3 | async-start | bytes 2359296 | tf_op jit(solution)/shard_map/all_to_all | solution.py:92
  273.1 46.9 %psum.14 = f32[192]{0:T(256)S(1)} all-reduce(f32[192]{0:T(256)S(1)} %get-tuple-element.29), channel_id=1, replica_groups=mesh['path'=48,'shard'=16] {'shard'}, use_global_device_ids=true, to_apply=%region_8.10 | all-reduce | flops 192 | bytes 1536 | tf_op jit(solution)/shard_map/psum | solution.py:126
  324.5 2.4 constant_dynamic-update-slice_fusion
  326.8 3.1 multiply_convert_fusion
  333.6 13.4 %all-to-all-start.8 = ((bf16[48,44,256]{2,1,0:T(8,128)(2,1)}), bf16[48,44,256]{2,1,0:T(8,128)(2,1)}, u32[]{:S(2)}, u32[]{:S(2)}) async-start(bf16[48,44,256]{2,1,0:T(8,128)(2,1)} %reshape.147), calls=%async_computation.8 | async-start | bytes 2359296 | tf_op jit(solution)/shard_map/all_to_all | solution.py:107
  347.1 3.1 multiply_reduce_fusion.1
  350.1 44.7 %psum.15 = f32[192]{0:T(256)S(1)} all-reduce(f32[192]{0:T(256)S(1)} %get-tuple-element.31), channel_id=1, replica_groups=mesh['path'=48,'shard'=16] {'shard'}, use_global_device_ids=true, to_apply=%region_10.12 | all-reduce | flops 192 | bytes 1536 | tf_op jit(solution)/shard_map/psum | solution.py:132
  394.8 3.6 multiply_convert_fusion.1
  399.8 12.4 %all-to-all-start.6 = ((bf16[48,44,256]{2,1,0:T(8,128)(2,1)}), bf16[48,44,256]{2,1,0:T(8,128)(2,1)}, u32[]{:S(2)}, u32[]{:S(2)}) async-start(bf16[48,44,256]{2,1,0:T(8,128)(2,1)} %reshape.143), calls=%async_computation.6 | async-start | bytes 2359296 | tf_op jit(solution)/shard_map/all_to_all | solution.py:107
  413.3 40.6 %all-to-all-done.6 = bf16[48,44,256]{2,1,0:T(8,128)(2,1)} async-done(((bf16[48,44,256]{2,1,0:T(8,128)(2,1)}), bf16[48,44,256]{2,1,0:T(8,128)(2,1)}, u32[]{:S(2)}, u32[]{:S(2)}) %all-to-all-start.6) | async-done | bytes 1081376 | tf_op jit(solution)/shard_map/all_to_all | solution.py:107
  453.9 10.1 %all-to-all-start.9 = ((bf16[48,44,256]{2,1,0:T(8,128)(2,1)}), bf16[48,44,256]{2,1,0:T(8,128)(2,1)}, u32[]{:S(2)}, u32[]{:S(2)}) async-start(bf16[48,44,256]{2,1,0:T(8,128)(2,1)} %reshape.149), calls=%async_computation.9 | async-start | bytes 2359296 | tf_op jit(solution)/shard_map/all_to_all | solution.py:107
  465.1 40.2 %all-to-all-done.9 = bf16[48,44,256]{2,1,0:T(8,128)(2,1)} async-done(((bf16[48,44,256]{2,1,0:T(8,128)(2,1)}), bf16[48,44,256]{2,1,0:T(8,128)(2,1)}, u32[]{:S(2)}, u32[]{:S(2)}) %all-to-all-start.9) | async-done | bytes 1081376 | tf_op jit(solution)/shard_map/all_to_all | solution.py:107
  505.4 10.1 %all-to-all-start.7 = ((bf16[48,44,256]{2,1,0:T(8,128)(2,1)}), bf16[48,44,256]{2,1,0:T(8,128)(2,1)S(1)}, u32[]{:S(2)}, u32[]{:S(2)}) async-start(bf16[48,44,256]{2,1,0:T(8,128)(2,1)} %reshape.145), calls=%async_computation.7 | async-start | bytes 2359296 | tf_op jit(solution)/shard_map/all_to_all | solution.py:107
  520.7 36.1 %all-to-all-done.7 = bf16[48,44,256]{2,1,0:T(8,128)(2,1)S(1)} async-done(((bf16[48,44,256]{2,1,0:T(8,128)(2,1)}), bf16[48,44,256]{2,1,0:T(8,128)(2,1)S(1)}, u32[]{:S(2)}, u32[]{:S(2)}) %all-to-all-start.7) | async-done | bytes 1081376 | tf_op jit(solution)/shard_map/all_to_all | solution.py:107
  (92 shorter events, 43.6 us)
Async XLA Ops:
  0.6 2.8 copy-start
  5.0 18.9 %copy-start.10 = (bf16[192,2112]{1,0:T(8,128)(2,1)S(1)}, bf16[192,2112]{1,0:T(8,128)(2,1)}, u32[]{:S(2)}) copy-start(bf16[192,2112]{1,0:T(8,128)(2,1)} %param.11) | copy-start | bytes 2433028
  5.0 50.1 %all-to-all-start.1 = ((bf16[48,4,2112]{2,1,0:T(4,128)(2,1)}), bf16[48,4,2112]{2,1,0:T(4,128)(2,1)S(1)}, u32[]{:S(2)}, u32[]{:S(2)}) async-start(bf16[48,4,2112]{2,1,0:T(4,128)(2,1)} %all_to_all.56), calls=%async_computation.1 | async-start | bytes 1671168 | tf_op jit(solution)/shard_map/all_to_all | solution.py:79
  25.4 40.4 %copy-start.6 = (f32[4,44,512]{2,0,1:T(4,128)S(1)}, f32[4,44,512]{2,0,1:T(4,128)}, u32[]{:S(2)}) copy-start(f32[4,44,512]{2,0,1:T(4,128)} %param.17) | copy-start | bytes 1081348
  25.4 40.5 %copy-start.14 = (s32[48,2]{0,1:T(2,128)S(1)}, s32[48,2]{0,1:T(2,128)}, u32[]{:S(2)}) copy-start(s32[48,2]{0,1:T(2,128)} %param.15) | copy-start | bytes 1156
  55.1 0.9 copy-start.5
  56.0 40.5 %all-to-all-start = ((bf16[48,4,2112]{2,1,0:T(4,128)(2,1)}), bf16[48,4,2112]{2,1,0:T(4,128)(2,1)S(1)}, u32[]{:S(2)}, u32[]{:S(2)}) async-start(bf16[48,4,2112]{2,1,0:T(4,128)(2,1)} %all_to_all.54), calls=%async_computation | async-start | bytes 1671168 | tf_op jit(solution)/shard_map/all_to_all | solution.py:78
  96.5 9.9 %copy-start.8 = (f32[4,44,512]{2,0,1:T(4,128)S(1)}, f32[4,44,512]{2,0,1:T(4,128)}, u32[]{:S(2)}) copy-start(f32[4,44,512]{2,0,1:T(4,128)} %param.16) | copy-start | bytes 1081348
  96.5 51.4 %all-to-all-start.2 = ((bf16[48,44,256]{2,1,0:T(8,128)(2,1)}), bf16[48,44,256]{2,1,0:T(8,128)(2,1)}, u32[]{:S(2)}, u32[]{:S(2)}) async-start(bf16[48,44,256]{2,1,0:T(8,128)(2,1)} %get-tuple-element.26), calls=%async_computation.2 | async-start | bytes 2359296 | tf_op jit(solution)/shard_map/all_to_all | solution.py:92
  148.0 51.3 %copy-start.2 = (bf16[48,44,256]{2,1,0:T(8,128)(2,1)S(1)}, bf16[48,44,256]{2,1,0:T(8,128)(2,1)}, u32[]{:S(2)}) copy-start(bf16[48,44,256]{2,1,0:T(8,128)(2,1)} %get-tuple-element.28) | copy-start | bytes 3244036
  250.6 71.7 %all-to-all-start.3 = ((bf16[48,44,256]{2,1,0:T(8,128)(2,1)}), bf16[48,44,256]{2,1,0:T(8,128)(2,1)}, u32[]{:S(2)}, u32[]{:S(2)}) async-start(bf16[48,44,256]{2,1,0:T(8,128)(2,1)} %get-tuple-element.25), calls=%async_computation.3 | async-start | bytes 2359296 | tf_op jit(solution)/shard_map/all_to_all | solution.py:92
  269.9 1.6 copy-start.3
  271.5 1.5 copy-start.1
  324.5 2.4 copy-start.11
  333.6 66.2 %all-to-all-start.8 = ((bf16[48,44,256]{2,1,0:T(8,128)(2,1)}), bf16[48,44,256]{2,1,0:T(8,128)(2,1)}, u32[]{:S(2)}, u32[]{:S(2)}) async-start(bf16[48,44,256]{2,1,0:T(8,128)(2,1)} %reshape.147), calls=%async_computation.8 | async-start | bytes 2359296 | tf_op jit(solution)/shard_map/all_to_all | solution.py:107
  399.8 12.4 %copy-start.4 = (bf16[2112,256]{1,0:T(8,128)(2,1)S(1)}, bf16[2112,256]{1,0:T(8,128)(2,1)}, u32[]{:S(2)}) copy-start(bf16[2112,256]{1,0:T(8,128)(2,1)} %get-tuple-element.10) | copy-start | bytes 3244036
  399.8 54.2 %all-to-all-start.6 = ((bf16[48,44,256]{2,1,0:T(8,128)(2,1)}), bf16[48,44,256]{2,1,0:T(8,128)(2,1)}, u32[]{:S(2)}, u32[]{:S(2)}) async-start(bf16[48,44,256]{2,1,0:T(8,128)(2,1)} %reshape.143), calls=%async_computation.6 | async-start | bytes 2359296 | tf_op jit(solution)/shard_map/all_to_all | solution.py:107
  453.9 51.4 %all-to-all-start.9 = ((bf16[48,44,256]{2,1,0:T(8,128)(2,1)}), bf16[48,44,256]{2,1,0:T(8,128)(2,1)}, u32[]{:S(2)}, u32[]{:S(2)}) async-start(bf16[48,44,256]{2,1,0:T(8,128)(2,1)} %reshape.149), calls=%async_computation.9 | async-start | bytes 2359296 | tf_op jit(solution)/shard_map/all_to_all | solution.py:107
  505.4 51.4 %all-to-all-start.7 = ((bf16[48,44,256]{2,1,0:T(8,128)(2,1)}), bf16[48,44,256]{2,1,0:T(8,128)(2,1)S(1)}, u32[]{:S(2)}, u32[]{:S(2)}) async-start(bf16[48,44,256]{2,1,0:T(8,128)(2,1)} %reshape.145), calls=%async_computation.7 | async-start | bytes 2359296 | tf_op jit(solution)/shard_map/all_to_all | solution.py:107
  518.9 38.2 %copy-start.7 = (f32[4,44,512]{2,0,1:T(4,128)S(1)}, f32[4,44,512]{2,0,1:T(4,128)}, u32[]{:S(2)}) copy-start(f32[4,44,512]{2,0,1:T(4,128)} %param.17) | copy-start | bytes 1081348
  518.9 38.2 %copy-start.12 = (bf16[4,44,512]{2,0,1:T(4,128)(2,1)S(1)}, bf16[4,44,512]{2,0,1:T(4,128)(2,1)}, u32[]{:S(2)}) copy-start(bf16[4,44,512]{2,0,1:T(4,128)(2,1)} %param.19) | copy-start | bytes 540676
  556.8 1.5 copy-start.9
  556.8 1.5 copy-start.13
where the time goes:
time: 566 us; the launch traced here: 559 us
  waiting for transfers between devices  208 us (37%)
  blocking collectives  194 us (34%)
  starting transfers between devices  94.7 us (17%)
  local copies, waits for them, and re-layouts  33.5 us (6%)
  matrix products  17.6 us (3%)
  other arithmetic  10.7 us (2%)
    all_to_all x4, waiting for transfers between devices, ship(): lax.all_to_all(outgoing, 'path', split_axis=0, concat_axis=0, tiled=True)  117 us
    all_to_all x2, blocking collectives, fetch(): lax.all_to_all(outgoing, 'path', split_axis=0, concat_axis=1, tiled=True)  103 us
    psum x1, blocking collectives, on_device(): squares = lax.psum(jnp.sum(activated * activated, axis=1), 'shard')  46.9 us
    all_to_all x4, starting transfers between devices, ship(): lax.all_to_all(outgoing, 'path', split_axis=0, concat_axis=0, tiled=True)  46 us
    psum x1, blocking collectives, on_device(): products = lax.psum(jnp.sum(back * hidden, axis=1), 'shard')  44.7 us
    all_to_all x2, waiting for transfers between devices, fetch(): lax.all_to_all(outgoing, 'path', split_axis=0, concat_axis=1, tiled=True)  36 us
    all_to_all x1, waiting for transfers between devices, on_device(): lax.all_to_all(sent_grads, 'path', split_axis=0, concat_axis=0, tiled=True)  29.7 us
    all_to_all x1, waiting for transfers between devices, on_device(): lax.all_to_all(sent_rows, 'path', split_axis=0, concat_axis=0, tiled=True)  25.2 us
  transfers between devices with their start and end apart: 8, of which 6 were waited for; matrix products, arithmetic and copies ran while one was open for 7% of the time, Pallas kernels for 0%

commit v1 on v0

v1 whole, which is shorter than its diff:
```python
import functools

import jax
import jax.numpy as jnp
from jax import lax
from jax.experimental import pallas as pl
from jax.experimental.pallas import tpu as pltpu
from jax.sharding import PartitionSpec as P

MESH = pl.DeviceIdType.MESH
BF = jnp.bfloat16
F32 = jnp.float32

FF = 8192
NZ = 12
NYL = 4
NY = 8
NX = 4
UNIT = 16
HALF = 1152
OFFS = (0, -1, 1, -2, 2, -3, 3, -4)

norm_epsilon = 1e-06
hidden_epsilon = 1e-05
adam_epsilon = 0.001
inner_rate = 0.05
decay_rate = 0.1
outer_rate = 0.7
momentum_coef = 0.9
gelu_coef = 0.7978845608
cubic_coef = 0.044715


def gelu_pair(values):
    inner = gelu_coef * (values + cubic_coef * values * values * values)
    tangent = jnp.tanh(inner)
    activated = 0.5 * values * (1.0 + tangent)
    slopes = 0.5 * (1.0 + tangent) + 0.5 * values * (1.0 - tangent * tangent) * gelu_coef * (
        1.0 + 3.0 * cubic_coef * values * values
    )
    return (activated, slopes)


def placing_matrix(lengths, targets, row_count, path_count, capacity):
    ends = jnp.cumsum(lengths)
    row_ids = jnp.arange(row_count, dtype=jnp.int32)
    doc_of_row = jnp.sum((row_ids[:, None] >= ends[None, :]).astype(jnp.int32), axis=1)
    doc_hit = doc_of_row[:, None] == jnp.arange(lengths.shape[0], dtype=jnp.int32)[None, :]
    row_path = jnp.sum(jnp.where(doc_hit, targets[None, :], 0), axis=1)
    path_hit = (row_path[:, None] == jnp.arange(path_count, dtype=jnp.int32)[None, :]).astype(
        jnp.int32
    )
    ranks = jnp.sum((jnp.cumsum(path_hit, axis=0) - 1) * path_hit, axis=1)
    slots = jnp.where(ranks < capacity, row_path * capacity + ranks, -1)
    return (jnp.arange(path_count * capacity, dtype=jnp.int32)[:, None] == slots[None, :]).astype(
        jnp.bfloat16
    )


def adam_delta(gradient, weight):
    update = gradient / (jnp.abs(gradient) + adam_epsilon) + decay_rate * weight.astype(jnp.float32)
    return (-inner_rate * update).astype(jnp.bfloat16)


def outer_update(master, moment, summed, counts):
    pseudo = -summed / jnp.maximum(counts, 1.0)[:, None, None]
    buffer = momentum_coef * moment.astype(jnp.float32) + pseudo
    return (master - outer_rate * (pseudo + momentum_coef * buffer), buffer.astype(jnp.bfloat16))


def place():
    path = lax.axis_index("path")
    shard = lax.axis_index("shard")
    return path // NYL, path % NYL, shard // 8, (shard // 2) % NX, shard % 2


def device(z, y, x, core):
    return (z * NYL + y % NYL, ((y // NYL) * NX + x) * 2 + core)


def aligned(value, multiple):
    return pl.multiple_of(value, multiple)


def signal(to):
    pl.semaphore_signal(
        pltpu.get_barrier_semaphore(), inc=1, device_id=to, device_id_type=MESH
    )


def gather_kernel(
    rows_ref,
    wsend_ref,
    perm_ref,
    x_out,
    w_out,
    wrecv,
    unit,
    a_sem,
    e_sem,
    z_sem,
    y_sem,
    x_sem,
    f_sem,
    s_sem,
    l_sem,
):
    z, y_lo, y_hi, x, core = place()
    y = y_hi * NYL + y_lo
    row_block = aligned((x * NYL + y_lo) * 48, 16)

    def remote(src, dst, sems, to):
        return pltpu.make_async_remote_copy(
            src_ref=src,
            dst_ref=dst,
            send_sem=sems.at[0],
            recv_sem=sems.at[1],
            device_id=to,
            device_id_type=MESH,
        )

    def chunk(xx, yy):
        return x_out.at[
            core,
            pl.ds(aligned((xx * NYL + yy % NYL) * 48, 16), 48),
            pl.ds(aligned((yy // NYL) * HALF, 128), HALF),
        ]

    def slab(xx):
        return x_out.at[core, pl.ds(aligned(xx * 192, 16), 192), :]

    def wrows(level, zz, lanes):
        return w_out.at[level, pl.ds(aligned(zz * 176, 16), 176), lanes]

    x_right, x_left, x_far = (x + 1) % NX, (x + 3) % NX, (x + 2) % NX
    to_xr, to_xl = device(z, y, x_right, core), device(z, y, x_left, core)
    to_yr, to_yl = device(z, (y + 1) % NY, x, core), device(z, (y + 7) % NY, x, core)
    to_zr, to_zl = device((z + 1) % NZ, y, x, core), device((z + 11) % NZ, y, x, core)
    to_core = device(z, y, x, 1 - core)
    group = [y_hi * NYL + (y_lo + step) % NYL for step in (1, 2, 3)]

    for to in (to_xr, to_xl, to_yr, to_yl, to_zr, to_zl, to_core):
        signal(to)
    for other in group:
        signal(device(z, other, x, core))
    for j in (1, 2):
        signal(device((z + 2 * NZ - x - 4 * j) % NZ, y, x, core))

    signal(device((z + NZ - jnp.where(x == 0, 6, x)) % NZ, y, x, core))
    pl.semaphore_wait(pltpu.get_barrier_semaphore(), 13)

    trades = []
    for level in range(2):
        for step in (1, 2, 3):
            other = (y_lo + step) % NYL
            copy = remote(
                wsend_ref.at[level, other],
                wrecv.at[level, y_lo],
                e_sem.at[level, step - 1],
                device(z, y_hi * NYL + other, x, core),
            )
            copy.start()
            trades.append(copy)
        wrecv[level, y_lo] = wsend_ref[level, y_lo]

    routed = []
    for j in range(3):
        target = (z + x + 4 * j) % NZ
        routed.append(
            remote(
                rows_ref.at[pl.ds(aligned(target * UNIT, 16), UNIT), :],
                x_out.at[
                    core,
                    pl.ds(aligned(row_block + j * UNIT, 16), UNIT),
                    pl.ds(aligned(y_hi * HALF, 128), HALF),
                ],
                a_sem.at[j],
                device(target, y, x, core),
            )
        )
    routed[1].start()
    routed[2].start()

    @pl.when(x == 0)
    def _():
        pltpu.make_async_copy(
            rows_ref.at[pl.ds(aligned(z * UNIT, 16), UNIT), :],
            x_out.at[
                core,
                pl.ds(row_block, UNIT),
                pl.ds(aligned(y_hi * HALF, 128), HALF),
            ],
            l_sem.at[2],
        ).start()

    @pl.when(x != 0)
    def _():
        routed[0].start()

    every = slice(0, 512)
    zcopies = {}

    def z_send(level, t, lanes_right, lanes_left, src_unit):
        for side, (to, sign, lanes) in enumerate(
            ((to_zr, -1, lanes_right), (to_zl, 1, lanes_left))
        ):
            zz = (z + NZ + sign * t) % NZ
            dst = wrows(level, zz, lanes)
            copy = remote(unit.at[level] if src_unit else dst, dst, z_sem.at[level, t, side], to)
            copy.start()
            zcopies[level, t, side] = copy

    def z_step(level, t):
        zcopies[level, t - 1, 0].wait_recv()
        zcopies[level, t - 1, 1].wait_recv()
        if t < 5:
            z_send(level, t, every, every, False)
        else:
            z_send(level, t, slice(0, 256), slice(256, 512), False)

    locals_ = []
    for level in range(2):
        for copy in trades[3 * level : 3 * level + 3]:
            copy.wait_recv()
        pieces = wrecv[level].reshape(4 * 176, 128)
        for m in range(4):
            unit[level, :, m * 128 : (m + 1) * 128] = jnp.dot(
                perm_ref[m * 176 : (m + 1) * 176, :], pieces, preferred_element_type=F32
            ).astype(BF)
        z_send(level, 0, every, every, True)
        copy = pltpu.make_async_copy(unit.at[level], wrows(level, z, every), l_sem.at[level])
        copy.start()
        locals_.append(copy)

    routed[1].wait_recv()
    routed[2].wait_recv()

    @pl.when(x == 0)
    def _():
        pltpu.make_async_copy(
            rows_ref.at[pl.ds(aligned(z * UNIT, 16), UNIT), :],
            x_out.at[
                core,
                pl.ds(row_block, UNIT),
                pl.ds(aligned(y_hi * HALF, 128), HALF),
            ],
            l_sem.at[2],
        ).wait()

    @pl.when(x != 0)
    def _():
        routed[0].wait_recv()

    ycopies = {}
    xcopies = {}
    fcopies = {}
    scopies = []

    def y_send(t):
        for side, (to, sign) in enumerate(((to_yr, -1), (to_yl, 1))):
            if side == 1 and t == 3:
                continue
            ref = chunk(x, (y + NY + sign * t) % NY)
            copy = remote(ref, ref, y_sem.at[t, side], to)
            copy.start()
            ycopies[t, side] = copy

    def x_send(n):
        ref = chunk(x, (y + NY + OFFS[n]) % NY)
        for side, to in enumerate((to_xr, to_xl)):
            copy = remote(ref, ref, x_sem.at[n, side], to)
            copy.start()
            xcopies[n, side] = copy

    def x_forward(n):
        side = n % 2
        xcopies[n, side].wait_recv()
        ref = chunk(x_left if side == 0 else x_right, (y + NY + OFFS[n]) % NY)
        copy = remote(ref, ref, f_sem.at[n], to_xr if side == 0 else to_xl)
        copy.start()
        fcopies[n] = copy

    def core_send(index, xx):
        copy = remote(slab(xx), slab(xx), s_sem.at[index], to_core)
        copy.start()
        scopies.append(copy)

    y_send(0)
    x_send(0)
    for t in range(1, 4):
        ycopies[t - 1, 0].wait_recv()
        ycopies[t - 1, 1].wait_recv()
        y_send(t)
        x_send(2 * t - 1)
        x_send(2 * t)
        if t >= 2:
            z_step(t - 2, 1)
    ycopies[3, 0].wait_recv()
    x_send(7)
    core_send(0, x)
    for n in range(4):
        x_forward(n)
    z_step(0, 2)
    z_step(1, 2)
    for n in range(4, 8):
        x_forward(n)
    for n in range(8):
        xcopies[n, 1 - n % 2].wait_recv()
    core_send(1, x_left)
    core_send(2, x_right)
    z_step(0, 3)
    z_step(1, 3)
    for n in range(8):
        fcopies[n].wait_recv()
    core_send(3, x_far)
    for t in (4, 5):
        z_step(0, t)
        z_step(1, t)
    for copy in scopies:
        copy.wait_recv()
    for level in range(2):
        for side in range(2):
            zcopies[level, 5, side].wait_recv()

    for copy in trades + scopies:
        copy.wait_send()
    for copy in locals_:
        copy.wait()
    for table in (zcopies, ycopies, xcopies, fcopies):
        for copy in table.values():
            copy.wait_send()
    routed[1].wait_send()
    routed[2].wait_send()

    @pl.when(x != 0)
    def _():
        routed[0].wait_send()


def reduce_kernel(in_ref, out_ref, first, second, mid, a_sem, b_sem):
    z, y_lo, y_hi, x, core = place()
    y = y_hi * NYL + y_lo
    c = x * 2 + core
    ys = [(y + s) % NY for s in range(1, NY)]
    cs = [(c + s) % 8 for s in range(1, 8)]
    for other in ys:
        signal(device(z, other, x, core))
    for other in cs:
        signal(device(z, y, other // 2, other % 2))
    pl.semaphore_wait(pltpu.get_barrier_semaphore(), 14)

    def trade(src, slots, mine, sems, targets):
        copies = []
        for s, to in enumerate(targets):
            copy = pltpu.make_async_remote_copy(
                src_ref=src,
                dst_ref=slots.at[mine],
                send_sem=sems.at[s, 0],
                recv_sem=sems.at[s, 1],
                device_id=to,
                device_id_type=MESH,
            )
            copy.start()
            copies.append(copy)
        slots[mine] = src[...]
        for copy in copies:
            copy.wait_recv()
        total = slots[0]
        for i in range(1, 8):
            total += slots[i]
        return total, copies

    mid[...], one = trade(in_ref, first, y, a_sem, [device(z, o, x, core) for o in ys])
    out_ref[...], two = trade(
        mid, second, c, b_sem, [device(z, y, o // 2, o % 2) for o in cs]
    )
    for copy in one + two:
        copy.wait_send()


def ship_kernel(up_ref, down_ref, perm_ref, out_ref, recv, work, z_sem, e_sem):
    z, y_lo, y_hi, x, core = place()
    y = y_hi * NYL + y_lo
    to_z = (device((z + 1) % NZ, y, x, core), device((z + 11) % NZ, y, x, core))
    for to in to_z:
        signal(to)
    for step in (1, 2, 3):
        signal(device(z, y_hi * NYL + (y_lo + step) % NYL, x, core))
    pl.semaphore_wait(pltpu.get_barrier_semaphore(), 5)
    own = (up_ref, down_ref)
    halves = (slice(0, 256), slice(256, 512))
    copies = {}

    def send(src, level, t, side, lanes):
        copy = pltpu.make_async_remote_copy(
            src_ref=src,
            dst_ref=recv.at[level, side, t, :, lanes],
            send_sem=z_sem.at[level, t, side, 0],
            recv_sem=z_sem.at[level, t, side, 1],
            device_id=to_z[side],
            device_id_type=MESH,
        )
        copy.start()
        copies[level, t, side] = copy

    def rows(zz):
        return pl.ds(aligned(zz * 176, 16), 176)

    for level in range(2):
        for side in range(2):
            send(
                own[level].at[rows((z + 6) % NZ), halves[side]], level, 0, side, halves[side]
            )
    for t in range(1, 6):
        for level in range(2):
            for side in range(2):
                target = (z + (6 - t if side == 0 else NZ - 6 + t)) % NZ
                copies[level, t - 1, side].wait_recv()
                if t == 1:
                    lanes, rest = halves[side], halves[1 - side]
                    recv[level, side, 0, :, rest] = own[level][rows(target), rest]
                else:
                    lanes = slice(0, 512)
                recv[level, side, t - 1, :, lanes] = (
                    recv[level, side, t - 1, :, lanes].astype(F32)
                    + own[level][rows(target), lanes].astype(F32)
                ).astype(BF)
                send(recv.at[level, side, t - 1], level, t, side, slice(0, 512))

    trades = []
    for level in range(2):
        copies[level, 5, 0].wait_recv()
        copies[level, 5, 1].wait_recv()
        total = (
            own[level][rows(z), :].astype(F32)
            + recv[level, 0, 5].astype(F32)
            + recv[level, 1, 5].astype(F32)
        ).astype(BF)
        pieces = jnp.concatenate([total[:, m * 128 : (m + 1) * 128] for m in range(4)], axis=0)
        work[level] = (
            jnp.dot(perm_ref[...], pieces, preferred_element_type=F32)
            .astype(BF)
            .reshape(4, 176, 128)
        )
        for step in (1, 2, 3):
            other = (y_lo + step) % NYL
            copy = pltpu.make_async_remote_copy(
                src_ref=work.at[level, other],
                dst_ref=out_ref.at[level, y_lo],
                send_sem=e_sem.at[level, step - 1, 0],
                recv_sem=e_sem.at[level, step - 1, 1],
                device_id=device(z, y_hi * NYL + other, x, core),
                device_id_type=MESH,
            )
            copy.start()
            trades.append(copy)
        out_ref[level, y_lo] = work[level, y_lo]
    for copy in trades:
        copy.wait()
    for copy in copies.values():
        copy.wait_send()


VMEM = pl.BlockSpec(memory_space=pltpu.VMEM)
ANY = pl.BlockSpec(memory_space=pl.ANY)
DMA = pltpu.SemaphoreType.DMA


def gather(rows, weights, perm):
    return pl.pallas_call(
        gather_kernel,
        out_shape=(
            jax.ShapeDtypeStruct((2, 768, 2 * HALF), BF),
            jax.ShapeDtypeStruct((2, 2112, 512), BF),
        ),
        in_specs=[VMEM, VMEM, VMEM],
        out_specs=(ANY, ANY),
        scratch_shapes=[
            pltpu.VMEM((2, 4, 176, 128), BF),
            pltpu.VMEM((2, 176, 512), BF),
            DMA((3, 2)),
            DMA((2, 3, 2)),
            DMA((2, 6, 2, 2)),
            DMA((4, 2, 2)),
            DMA((8, 2, 2)),
            DMA((8, 2)),
            DMA((4, 2)),
            DMA((3,)),
        ],
        compiler_params=pltpu.CompilerParams(
            collective_id=0, has_side_effects=True, vmem_limit_bytes=48 * 1024 * 1024
        ),
        name="gather",
    )(rows, weights, perm)


def reduce_rows(sums):
    return pl.pallas_call(
        reduce_kernel,
        out_shape=jax.ShapeDtypeStruct((16, 128), F32),
        in_specs=[VMEM],
        out_specs=VMEM,
        scratch_shapes=[
            pltpu.VMEM((8, 16, 128), F32),
            pltpu.VMEM((8, 16, 128), F32),
            pltpu.VMEM((16, 128), F32),
            DMA((7, 2)),
            DMA((7, 2)),
        ],
        compiler_params=pltpu.CompilerParams(collective_id=1, has_side_effects=True),
        name="reduce_rows",
    )(sums)


def ship(up, down, perm):
    return pl.pallas_call(
        ship_kernel,
        out_shape=jax.ShapeDtypeStruct((2, 4, 176, 128), BF),
        in_specs=[VMEM, VMEM, VMEM],
        out_specs=VMEM,
        scratch_shapes=[
            pltpu.VMEM((2, 2, 6, 176, 512), BF),
            pltpu.VMEM((2, 4, 176, 128), BF),
            DMA((2, 6, 2, 2)),
            DMA((2, 3, 2)),
        ],
        compiler_params=pltpu.CompilerParams(
            collective_id=2, has_side_effects=True, vmem_limit_bytes=48 * 1024 * 1024
        ),
        name="ship",
    )(up, down, perm)


def on_device(
    tokens,
    out_grad,
    doc_lengths,
    doc_paths,
    membership,
    up_master,
    down_master,
    up_moment,
    down_moment,
):
    path_count = lax.axis_size("path")
    row_count, width = tokens.shape
    module_count, owner_rows, owner_columns = up_master.shape
    capacity = row_count // path_count
    z, y_lo, y_hi, x, core = place()

    placing = placing_matrix(doc_lengths[0], doc_paths[0], row_count, path_count, capacity)
    rows_float = tokens.astype(F32)
    normed = (
        rows_float
        * lax.rsqrt(jnp.mean(rows_float * rows_float, axis=1, keepdims=True) + norm_epsilon)
    ).astype(BF)
    chosen = jnp.where(core == 0, normed, out_grad)
    half = jnp.where(
        y_hi == 0,
        chosen[:, :HALF],
        jnp.pad(chosen[:, HALF:], ((0, 0), (0, 2 * HALF - width))),
    )
    rows = jnp.dot(placing, half, preferred_element_type=F32).astype(BF)

    def blocks(master):
        flat = master.astype(BF).reshape(module_count * owner_rows, NYL, 128)
        return flat.transpose(1, 0, 2)

    weights_out = jnp.stack([blocks(up_master), blocks(down_master)])
    index = jnp.arange(NYL * module_count * owner_rows, dtype=jnp.int32)
    m_of = index // (NYL * owner_rows)
    y_of = (index // owner_rows) % NYL
    source = (y_of * module_count + m_of) * owner_rows + index % owner_rows
    perm = (source[:, None] == index[None, :]).astype(BF)

    features, weights = gather(rows, weights_out, perm)
    normed_in = features[0, :, :width]
    grads_in = features[1, :, :width]
    up_weight, down_weight = weights[0], weights[1]

    plane_rows = features.shape[1]
    row_path = (jnp.arange(plane_rows, dtype=jnp.int32) // capacity) % NYL
    members = lax.dynamic_slice_in_dim(membership, z * NYL, NYL, 0)
    row_hit = row_path[:, None] == jnp.arange(NYL, dtype=jnp.int32)[None, :]
    row_module = jnp.sum(
        jnp.where(row_hit[:, :, None], members[None, :, :], 0), axis=1
    )

    def pick(product, level):
        out = 0.0
        for m in range(module_count):
            out = jnp.where(
                row_module[:, level : level + 1] == m, product[:, m * 128 : (m + 1) * 128], out
            )
        return out

    pre = pick(jnp.dot(normed_in, up_weight, preferred_element_type=F32), 0)
    back = pick(jnp.dot(grads_in, down_weight, preferred_element_type=F32), 1)
    activated, slopes = gelu_pair(pre)
    squares = jnp.sum(activated * activated, axis=1)
    products = jnp.sum(back * activated, axis=1)
    sums = jnp.concatenate(
        [squares.reshape(6, 128), products.reshape(6, 128), jnp.zeros((4, 128), F32)], axis=0
    )
    sums = reduce_rows(sums)
    scale = jnp.sqrt(sums[:6].reshape(plane_rows) / FF + hidden_epsilon)[:, None]
    mixing = sums[6:12].reshape(plane_rows)[:, None] / scale / FF
    hidden = activated / scale
    hidden_b = hidden.astype(BF)
    dpre = ((back - hidden * mixing) / scale * slopes).astype(BF)

    def spread(values):
        return jnp.concatenate(
            [jnp.where(row_hit[:, i : i + 1], values, 0) for i in range(NYL)], axis=1
        )

    def module_sums(left, right, weight, level):
        gradient = lax.dot_general(
            left, spread(right), (((0,), (0,)), ((), ())), preferred_element_type=F32
        )
        totals = [jnp.zeros((width, 128), F32) for _ in range(module_count)]
        for i in range(NYL):
            mine = weight[:, :128]
            for m in range(1, module_count):
                mine = jnp.where(members[i, level] == m, weight[:, m * 128 : (m + 1) * 128], mine)
            delta = adam_delta(gradient[:, i * 128 : (i + 1) * 128], mine).astype(F32)
            for m in range(module_count):
                totals[m] = totals[m] + jnp.where(members[i, level] == m, delta, 0.0)
        return jnp.concatenate(totals, axis=1).astype(BF)

    down_sums = module_sums(grads_in, hidden_b, down_weight, 1)
    up_sums = module_sums(normed_in, dpre, up_weight, 0)
    summed = ship(up_sums, down_sums, perm.T)

    module_ids = jnp.arange(module_count, dtype=jnp.int32)

    def update(master, moment, level):
        counts = jnp.sum((membership[:, level][None, :] == module_ids[:, None]).astype(F32), axis=1)
        total = (
            summed[level]
            .reshape(NYL, module_count, owner_rows, 128)
            .transpose(1, 2, 0, 3)
            .reshape(module_count, owner_rows, owner_columns)
        )
        return outer_update(master, moment, total.astype(F32), counts)

    new_up, new_up_moment = update(up_master, up_moment, 0)
    new_down, new_down_moment = update(down_master, down_moment, 1)
    return (new_up, new_down, new_up_moment, new_down_moment)


def solution(mesh):
    split = P(None, "path", "shard")
    rows = P("path", None)
    return jax.shard_map(
        on_device,
        mesh=mesh,
        in_specs=(rows, rows, rows, rows, P(), split, split, split, split),
        out_specs=(split, split, split, split),
        check_vma=False,
    )
```

time: 566 us -> 206 us (0.36)
  waiting for transfers between devices: 208 us -> 0 us
  blocking collectives: 194 us -> 0 us
  Pallas kernels: 0 us -> 146 us
  starting transfers between devices: 94.7 us -> 0 us
  local copies, waits for them, and re-layouts: 33.5 us -> 7.23 us
  between operations: 0.98 us -> 22.3 us
  matrix products: 17.6 us -> 10.8 us
  other arithmetic: 10.7 us -> 17.5 us
    all_to_all x8 -> x0, waiting for transfers between devices: 208 us -> none  [the longest x4 117 us: ship(): lax.all_to_all(outgoing, 'path', split_axis=0, concat_axis=0, tiled=True)]
    pallas_call x0 -> x3, Pallas kernels: none -> 146 us  [the longest x1 77 us: gather(): pl.pallas_call(gather_kernel, out_shape=(jax.ShapeDtypeStruct((2, 768, 2...]
    all_to_all x2 -> x0, blocking collectives: 103 us -> none  [fetch(): lax.all_to_all(outgoing, 'path', split_axis=0, concat_axis=1, tiled=True)]
    all_to_all x8 -> x0, starting transfers between devices: 94.7 us -> none  [the longest x4 46 us: ship(): lax.all_to_all(outgoing, 'path', split_axis=0, concat_axis=0, tiled=True)]
    psum x2 -> x0, blocking collectives: 91.6 us -> none  [the longest x1 46.9 us: on_device(): squares = lax.psum(jnp.sum(activated * activated, axis=1), 'shard')]
    squeeze x5 -> x1, local copies, waits for them, and re-layouts: 8.66 us -> 1.68 us  [on_device(): up_weight, down_weight = (weights[0], weights[1])]
    dot_general x10 -> x5, matrix products: 17.6 us -> 10.8 us  [the longest x2 6.16 us: module_sums(): lax.dot_general(left, spread(right), (((0,), (0,)), ((), ())), preferred_...]
    another operation x6 -> x11, other arithmetic: 0.89 us -> 7.13 us
  transfers between devices with their start and end apart: 8 -> 0, of which waited for: 6 -> 0; matrix products, arithmetic and copies ran while one was open for 7% -> 0% of each run, Pallas kernels for 0% -> 0%
where the time goes in v1:
time: 206 us; the launch traced here: 204 us
  Pallas kernels  146 us (71%)
  between operations  22.3 us (11%)
  other arithmetic  17.5 us (8%)
  matrix products  10.8 us (5%)
  local copies, waits for them, and re-layouts  7.23 us (4%)
    pallas_call x1, Pallas kernels, gather(): pl.pallas_call(gather_kernel, out_shape=(jax.ShapeDtypeStruct((2, 768, 2...  77 us
    pallas_call x1, Pallas kernels, ship(): pl.pallas_call(ship_kernel, out_shape=jax.ShapeDtypeStruct((2, 4, 176, 12...  54.9 us
    pallas_call x1, Pallas kernels, reduce_rows(): pl.pallas_call(reduce_kernel, out_shape=jax.ShapeDtypeStruct((16, 128), F...  14 us
    another operation x10, other arithmetic  7.09 us
    dot_general x2, matrix products, module_sums(): lax.dot_general(left, spread(right), (((0,), (0,)), ((), ())), preferred_...  6.16 us

profile of v1, /device:TPU:56, one launch (start us, length us, event | category | flops | bytes accessed | tf_op | source)
XLA Modules:
  0.0 203.8 jit_solution(14770485317765326907)
XLA Ops:
  0.6 0.8 slice_bitcast_fusion.2
  1.6 0.8 constant_dynamic-slice_fusion
  2.3 0.7 fusion.109
  5.5 1.4 fusion.14
  8.1 0.6 reduce-window.19
  10.9 77.0 %gather.1 = (bf16[2,768,2304]{2,1,0:T(8,128)(2,1)}, bf16[2,2112,512]{2,1,0:T(8,128)(2,1)S(1)}) custom-call(bf16[192,1152]{1,0:T(8,128)(2,1)S(1)} %convolution_convert_fusion.rows_ref, bf16[2,4,176,128]{3,2,1,0:T(8,128)(2,1)S(1)} %pad_maximum_fusion.2.wsend_ref, bf16[704,704]{1,0:T(8,128)(2,1)S(1)} %get-tuple-element.63.perm_ref), custom_call_target="tpu_custom_call" | custom-call | tf_op jit(solution)/shard_map/gather/pallas_call | solution.py:470
  88.0 1.7 slice_bitcast_fusion.1
  92.5 2.1 %fusion.2 = f32[768,512]{0,1:T(8,128)S(1)} fusion(bf16[2,768,2304]{2,1,0:T(8,128)(2,1)S(1)} %copy-done.10, bf16[2,2112,512]{2,1,0:T(8,128)(2,1)S(1)} %get-tuple-element.7), kind=kOutput, calls=%fused_computation.2 | convolution fusion | flops 1660944384 | bytes 7077888 | tf_op jit(solution)/shard_map/dot_general | solution.py:598
  94.8 2.1 %fusion.6 = f32[768,512]{0,1:T(8,128)S(1)} fusion(bf16[2,768,2304]{2,1,0:T(8,128)(2,1)S(1)} %copy-done.10, bf16[2,2112,512]{2,1,0:T(8,128)(2,1)S(1)} %get-tuple-element.7), kind=kOutput, calls=%fused_computation.6 | convolution fusion | flops 1660944384 | bytes 7077888 | tf_op jit(solution)/shard_map/dot_general | solution.py:597
  96.9 1.2 multiply_reduce_fusion.1
  98.2 0.7 maximum_maximum_fusion.in_ref
  98.9 14.0 %reduce_rows.1 = f32[16,128]{1,0:T(8,128)} custom-call(f32[16,128]{1,0:T(8,128)} %maximum_maximum_fusion.in_ref), custom_call_target="tpu_custom_call" | custom-call | tf_op jit(solution)/shard_map/reduce_rows/pallas_call | solution.py:498
  112.9 0.8 sqrt_bitcast_fusion
  113.7 1.5 broadcast_select_fusion.6
  115.3 4.1 %fusion.4 = f32[2112,512]{1,0:T(8,128)S(1)} fusion(bf16[2,768,2304]{2,1,0:T(8,128)(2,1)} %get-tuple-element.6, bf16[768,128]{0,1:T(8,128)(2,1)S(1)} %get-tuple-element.59, bf16[768,128]{0,1:T(8,128)(2,1)S(1)} %get-tuple-element.58, bf16[768,128]{0,1:T(8,128)(2,1)S(1)} %get-tuple-element.57, bf16[768,128]{0,1:T(8,128)(2,1)S(1)} %get-tuple-element.50), kind=kOutput, calls=%fused_computation.4 | convolution fusion | flops 1664090112 | bytes 8454144 | tf_op jit(solution)/shard_map/dot_general | solution.py:618
  125.1 2.2 %fusion.19 = (bf16[2112,128]{1,0:T(8,128)(2,1)S(1)}, bf16[2112,128]{1,0:T(8,128)(2,1)S(1)}, bf16[2112,128]{1,0:T(8,128)(2,1)S(1)}, bf16[2112,128]{1,0:T(8,128)(2,1)S(1)}, bf16[2112,128]{1,0:T(8,128)(2,1)S(1)}) fusion(pred[]{:T(512)} %bitcast.27, pred[]{:T(512)} %bitcast.23, pred[]{:T(512)} %bitcast.19, pred[]{:T(512)} %bitcast, ...), kind=kLoop, calls=%fused_computation.60 | loop fusion | flops 15138816 | bytes 9191440 | tf_op jit(solution)/shard_map/convert.7
  127.4 1.0 fusion.23
  133.2 2.0 fusion
  141.0 2.0 fusion.35
  143.0 1.0 fusion.39
  144.3 54.9 %ship.1 = bf16[2,4,176,128]{3,2,1,0:T(8,128)(2,1)S(1)} custom-call(bf16[2112,512]{1,0:T(8,128)(2,1)S(1)} %pad_maximum_fusion.up_ref, bf16[2112,512]{1,0:T(8,128)(2,1)S(1)} %pad_maximum_fusion.1.down_ref, bf16[704,704]{1,0:T(8,128)(2,1)S(1)} %get-tuple-element.62.perm_ref), custom_call_target="tpu_custom_call" | custom-call | tf_op jit(solution)/shard_map/ship/pallas_call | solution.py:516
  200.2 1.3 fusion.79
  201.8 0.7 copy-done.5
  202.5 1.3 fusion.78
  (71 shorter events, 5.6 us)
Async XLA Ops:
  0.6 6.3 %copy-start.1 = (bf16[192,2112]{1,0:T(8,128)(2,1)S(1)}, bf16[192,2112]{1,0:T(8,128)(2,1)}, u32[]{:S(2)}) copy-start(bf16[192,2112]{1,0:T(8,128)(2,1)} %param.9) | copy-start | bytes 2433028
  7.0 0.7 copy-start.8
  7.0 1.0 copy-start.9
  7.4 2.0 copy-start.4
  9.1 1.0 copy-start.2
  88.0 4.5 %copy-start.10 = (bf16[2,768,2304]{2,1,0:T(8,128)(2,1)S(1)}, bf16[2,768,2304]{2,1,0:T(8,128)(2,1)}, u32[]{:S(2)}) copy-start(bf16[2,768,2304]{2,1,0:T(8,128)(2,1)} %get-tuple-element.6) | copy-start | bytes 21233668
  115.3 9.8 %copy-start = (bf16[2112,512]{1,0:T(8,128)(2,1)S(1)}, bf16[2112,512]{1,0:T(8,128)(2,1)}, u32[]{:S(2)}) copy-start(bf16[2112,512]{1,0:T(8,128)(2,1)} %get-tuple-element.39) | copy-start | bytes 6488068
  115.3 17.8 %slice-start = ((s8[7077888]{0:T(1024)(128)(4,1)}), s8[2883584]{0:T(1024)(128)(4,1)S(1)}, s32[]{:S(2)}) async-start(s8[7077888]{0:T(1024)(128)(4,1)} %bitcast.92), calls=%async_computation | async-start | bytes 5767168
  125.1 8.0 %slice-start.1 = ((s8[7077888]{0:T(1024)(128)(4,1)}), s8[4194304]{0:T(1024)(128)(4,1)S(1)}, s32[]{:S(2)}) async-start(s8[7077888]{0:T(1024)(128)(4,1)} %bitcast.92), calls=%async_computation.1 | async-start | bytes 8388608
  199.2 1.0 copy-start.3
  199.2 1.0 copy-start.6
  201.5 1.0 copy-start.5
  201.5 1.0 copy-start.7

commit v2 on v0

v2 whole, which is shorter than its diff:
```python
import functools

import jax
import jax.numpy as jnp
from jax import lax
from jax.experimental import pallas as pl
from jax.experimental.pallas import tpu as pltpu
from jax.sharding import PartitionSpec as P

MESH = pl.DeviceIdType.MESH
BF = jnp.bfloat16
F32 = jnp.float32

FF = 8192
NZ = 12
NYL = 4
NY = 8
NX = 4
UNIT = 16
HALF = 1152
WIDE = 2304
BLOCK = 192
USED = 176
PLANE = 768
OFFS = (0, -1, 1, -2, 2, -3, 3, -4)

norm_epsilon = 1e-06
hidden_epsilon = 1e-05
adam_epsilon = 0.001
inner_rate = 0.05
decay_rate = 0.1
outer_rate = 0.7
momentum_coef = 0.9
gelu_coef = 0.7978845608
cubic_coef = 0.044715


def gelu_pair(values):
    inner = gelu_coef * (values + cubic_coef * values * values * values)
    tangent = jnp.tanh(inner)
    activated = 0.5 * values * (1.0 + tangent)
    slopes = 0.5 * (1.0 + tangent) + 0.5 * values * (1.0 - tangent * tangent) * gelu_coef * (
        1.0 + 3.0 * cubic_coef * values * values
    )
    return (activated, slopes)


def placing_matrix(lengths, targets, row_count, path_count, capacity):
    ends = jnp.cumsum(lengths)
    row_ids = jnp.arange(row_count, dtype=jnp.int32)
    doc_of_row = jnp.sum((row_ids[:, None] >= ends[None, :]).astype(jnp.int32), axis=1)
    doc_hit = doc_of_row[:, None] == jnp.arange(lengths.shape[0], dtype=jnp.int32)[None, :]
    row_path = jnp.sum(jnp.where(doc_hit, targets[None, :], 0), axis=1)
    path_hit = (row_path[:, None] == jnp.arange(path_count, dtype=jnp.int32)[None, :]).astype(
        jnp.int32
    )
    ranks = jnp.sum((jnp.cumsum(path_hit, axis=0) - 1) * path_hit, axis=1)
    slots = jnp.where(ranks < capacity, row_path * capacity + ranks, -1)
    return (jnp.arange(path_count * capacity, dtype=jnp.int32)[:, None] == slots[None, :]).astype(
        jnp.bfloat16
    )


def adam_delta(gradient, weight):
    update = gradient / (jnp.abs(gradient) + adam_epsilon) + decay_rate * weight.astype(jnp.float32)
    return (-inner_rate * update).astype(jnp.bfloat16)


def outer_update(master, moment, summed, counts):
    pseudo = -summed / jnp.maximum(counts, 1.0)[:, None, None]
    buffer = momentum_coef * moment.astype(jnp.float32) + pseudo
    return (master - outer_rate * (pseudo + momentum_coef * buffer), buffer.astype(jnp.bfloat16))


def place():
    path = lax.axis_index("path")
    shard = lax.axis_index("shard")
    return path // NYL, path % NYL, shard // 8, (shard // 2) % NX, shard % 2


def device(z, y, x, core):
    return (z * NYL + y % NYL, ((y // NYL) * NX + x) * 2 + core)


def aligned(value, multiple):
    return pl.multiple_of(value, multiple)


def signal(to):
    pl.semaphore_signal(
        pltpu.get_barrier_semaphore(), inc=1, device_id=to, device_id_type=MESH
    )


def fused_kernel(
    rows_ref,
    wsend_ref,
    mask_ref,
    pick_ref,
    out_ref,
    xs,
    xt,
    up_w,
    down_w,
    grads,
    up_p,
    down_p,
    act_ref,
    slope_ref,
    back_ref,
    scale_ref,
    spread_ref,
    perm_ref,
    wrecv,
    unit,
    recv,
    work,
    sums_ref,
    mid_ref,
    slots,
    a_sem,
    e_sem,
    z_sem,
    r_sem,
    ax_sem,
    ay_sem,
    by_sem,
    bx_sem,
    f_sem,
    s_sem,
    t_sem,
    o_sem,
    l_sem,
):
    z, y_lo, y_hi, x, core = place()
    y = y_hi * NYL + y_lo
    c = x * 2 + core
    weights = (up_w, down_w)
    parts = (up_p, down_p)

    def remote(src, dst, sems, to):
        return pltpu.make_async_remote_copy(
            src_ref=src,
            dst_ref=dst,
            send_sem=sems.at[0],
            recv_sem=sems.at[1],
            device_id=to,
            device_id_type=MESH,
        )

    started = []

    def start(src, dst, sems, to):
        copy = remote(src, dst, sems, to)
        copy.start()
        started.append(copy)
        return copy

    x_right, x_left, x_far = (x + 1) % NX, (x + 3) % NX, (x + 2) % NX
    to_x = (device(z, y, x_right, core), device(z, y, x_left, core))
    to_y = (device(z, (y + 1) % NY, x, core), device(z, (y + 7) % NY, x, core))
    to_z = (device((z + 1) % NZ, y, x, core), device((z + 11) % NZ, y, x, core))
    to_core = device(z, y, x, 1 - core)
    all_y = [device(z, (y + s) % NY, x, core) for s in range(1, NY)]
    all_c = [device(z, y, ((c + s) % 8) // 2, (c + s) % 2) for s in range(1, 8)]

    for to in all_y + all_c:
        signal(to)
    for to in to_z:
        signal(to)
    for j in (1, 2):
        signal(device((z + 2 * NZ - x - 4 * j) % NZ, y, x, core))
    signal(device((z + NZ - jnp.where(x == 0, 6, x)) % NZ, y, x, core))
    pl.semaphore_wait(pltpu.get_barrier_semaphore(), 19)

    half_cols = pl.ds(aligned(y_hi * HALF, 128), HALF)

    def trade_columns(level):
        copies = []
        for step in (1, 2, 3):
            other = (y_lo + step) % NYL
            copies.append(
                start(
                    wsend_ref.at[level, other],
                    wrecv.at[level, y_lo],
                    e_sem.at[level, step - 1],
                    device(z, y_hi * NYL + other, x, core),
                )
            )
        wrecv[level, y_lo] = wsend_ref[level, y_lo]
        return copies

    trades = [trade_columns(0)]
    b_row = 256 + (x * NYL + y_lo) * 32
    landing = [
        xs.at[core, pl.ds(aligned((y_lo * NX + x) * UNIT, 16), UNIT), half_cols],
        xs.at[core, pl.ds(aligned(b_row, 16), UNIT), half_cols],
        xs.at[core, pl.ds(aligned(b_row + UNIT, 16), UNIT), half_cols],
    ]
    routed = []
    for j in range(3):
        target = (z + x + 4 * j) % NZ
        routed.append(
            remote(
                rows_ref.at[pl.ds(aligned(target * UNIT, 16), UNIT), :],
                landing[j],
                a_sem.at[j],
                device(target, y, x, core),
            )
        )
    own_rows = pltpu.make_async_copy(
        rows_ref.at[pl.ds(aligned(z * UNIT, 16), UNIT), :], landing[0], l_sem
    )
    routed[1].start()
    routed[2].start()

    @pl.when(x == 0)
    def _():
        own_rows.start()

    @pl.when(x != 0)
    def _():
        routed[0].start()

    trades.append(trade_columns(1))

    for level in range(2):
        for zz in range(NZ):
            weights[level][zz * BLOCK + USED : (zz + 1) * BLOCK, :] = jnp.zeros(
                (BLOCK - USED, 512), BF
            )
    sums_ref[...] = jnp.zeros_like(sums_ref)

    def fill_perm(i, carry):
        shape = (16, 704)
        a = lax.broadcasted_iota(jnp.int32, shape, 0) + i * 16
        b = lax.broadcasted_iota(jnp.int32, shape, 1)
        first = sum((a >= 176 * k).astype(jnp.int32) for k in (1, 2, 3))
        rest = a - 176 * first
        second = sum((rest >= 44 * k).astype(jnp.int32) for k in (1, 2, 3))
        perm_ref[pl.ds(aligned(i * 16, 16), 16), :] = jnp.where(
            b == a + 132 * (second - first), 1.0, 0.0
        ).astype(BF)
        return carry

    lax.fori_loop(0, 44, fill_perm, 0)

    zcopies = {}

    def wblock(level, zz, h):
        return weights[level].at[
            pl.ds(aligned(zz * BLOCK, 16), USED), h * 256 : (h + 1) * 256
        ]

    def z_send(level, t, side, h):
        zz = (z + NZ + (-t if side == 0 else t)) % NZ
        dst = wblock(level, zz, h)
        zcopies[level, t, side, h] = start(dst, dst, z_sem.at[level, t, side, h], to_z[side])

    def z_first(level):
        for copy in trades[level]:
            copy.wait_recv()
        pieces = wrecv[level].reshape(4 * USED, 128)
        for m in range(4):
            weights[level][pl.ds(aligned(z * BLOCK, 16), USED), m * 128 : (m + 1) * 128] = jnp.dot(
                perm_ref[m * USED : (m + 1) * USED, :], pieces, preferred_element_type=F32
            ).astype(BF)
        for h in range(2):
            for side in range(2):
                z_send(level, 0, side, h)

    def z_step(level, t):
        for h in range(2):
            for side in range(2):
                zcopies[level, t - 1, side, h].wait_recv()
                if t < 5 or h == side:
                    z_send(level, t, side, h)

    def z_last(level):
        for side in range(2):
            zcopies[level, 5, side, side].wait_recv()

    def a_unit(xx):
        return xs.at[core, pl.ds(aligned((y_lo * NX + xx) * UNIT, 16), UNIT), half_cols]

    def cols_of(yy):
        return pl.ds(aligned((yy // NYL) * HALF, 128), HALF)

    def a_block(yy):
        return xs.at[core, pl.ds(aligned((yy % NYL) * 64, 16), 64), cols_of(yy)]

    def b_chunk(xx, yy):
        return xs.at[
            core, pl.ds(aligned(256 + (xx * NYL + yy % NYL) * 32, 16), 32), cols_of(yy)
        ]

    def b_slab(xx):
        return xs.at[core, pl.ds(aligned(256 + xx * 128, 16), 128), :]

    ycopies = {}

    def y_send(block, name, sems, t):
        for side in range(2 if t < 3 else 1):
            yy = (y + NY + (-t if side == 0 else t)) % NY
            ref = block(yy)
            ycopies[name, t, side] = start(ref, ref, sems.at[t, side], to_y[side])

    def y_wait(name, t):
        for side in range(2 if t < 3 else 1):
            ycopies[name, t, side].wait_recv()

    def b_y_send(t):
        y_send(lambda yy: b_chunk(x, yy), "b", by_sem, t)

    def a_y_send(t):
        y_send(a_block, "a", ay_sem, t)

    xcopies = {}
    fcopies = {}
    scopies = []

    def b_x_send(n):
        ref = b_chunk(x, (y + NY + OFFS[n]) % NY)
        for side in range(2):
            xcopies[n, side] = start(ref, ref, bx_sem.at[n, side], to_x[side])

    def b_forward(n):
        side = n % 2
        xcopies[n, side].wait_recv()
        ref = b_chunk((x_left, x_right)[side], (y + NY + OFFS[n]) % NY)
        fcopies[n] = start(ref, ref, f_sem.at[n], to_x[side])

    def core_send(index, ref):
        scopies.append(start(ref, ref, s_sem.at[index], to_core))

    tcopies = {}

    def sums_send(which, stage):
        src = (sums_ref, mid_ref)[stage].at[which]
        mine = (y, c)[stage]
        tcopies[which, stage] = [
            start(src, slots.at[which, stage, mine], t_sem.at[which, stage, s], to)
            for s, to in enumerate((all_y, all_c)[stage])
        ]
        slots[which, stage, mine] = src[...]

    def sums_wait(which, stage):
        for copy in tcopies[which, stage]:
            copy.wait_recv()
        total = slots[which, stage, 0]
        for i in range(1, 8):
            total += slots[which, stage, i]
        return total

    def picked(product, level):
        masked = product.reshape(12, 16, 512) * mask_ref[level][None]
        total = masked[:, :, :128]
        for m in range(1, 4):
            total = total + masked[:, :, m * 128 : (m + 1) * 128]
        return total.reshape(BLOCK, 128)

    def forward(first, last):
        def body(i, carry):
            here = pl.ds(aligned(i * BLOCK, 16), BLOCK)
            pre = picked(jnp.dot(xs[0, here, :], up_w[...], preferred_element_type=F32), 0)
            act_ref[here, :], slope_ref[here, :] = gelu_pair(pre)
            return carry

        lax.fori_loop(first, last, body, 0)

    def backward(first, last):
        def body(i, carry):
            here = pl.ds(aligned(i * BLOCK, 16), BLOCK)
            back_ref[here, :] = picked(
                jnp.dot(xs[1, here, :], down_w[...], preferred_element_type=F32), 1
            )
            return carry

        lax.fori_loop(first, last, body, 0)

    def row_sums(which, left, right):
        for k in range(6):
            here = slice(k * 128, (k + 1) * 128)
            sums_ref[which, k : k + 1, :] = jnp.sum(
                (left[here, :] * right[here, :]).T, axis=0, keepdims=True
            )

    def column(row):
        return jnp.broadcast_to(row, (128, 128)).T

    def store_spread(k, values):
        here = slice(k * 128, (k + 1) * 128)
        path = (lax.broadcasted_iota(jnp.int32, (128, 128), 0) // 4) % 4
        for i in range(4):
            spread_ref[here, i * 128 : (i + 1) * 128] = jnp.where(path == i, values, 0.0).astype(BF)

    def make_hidden(total):
        scale_row = jnp.sqrt(total / FF + hidden_epsilon)
        for k in range(6):
            here = slice(k * 128, (k + 1) * 128)
            scale = column(scale_row[k : k + 1, :])
            scale_ref[here, :] = scale
            hidden = act_ref[here, :] / scale
            act_ref[here, :] = hidden
            store_spread(k, hidden)

    def make_dpre(total):
        mix_row = total / FF
        for k in range(6):
            here = slice(k * 128, (k + 1) * 128)
            mixing = column(mix_row[k : k + 1, :])
            hidden = act_ref[here, :]
            store_spread(
                k,
                (back_ref[here, :] - hidden * mixing) / scale_ref[here, :] * slope_ref[here, :],
            )

    def turn(which, first, last):
        def body(i, carry):
            here = pl.ds(aligned(i * 128, 128), 128)
            xt[which, here, :] = xs[which, :, here].T
            return carry

        lax.fori_loop(first, last, body, 0)

    def gradient(which, first, last):
        def body(i, carry):
            here = pl.ds(aligned(i * 384, 128), 384)
            grads[here, :] = jnp.dot(
                xt[which, here, :], spread_ref[...], preferred_element_type=F32
            )
            return carry

        lax.fori_loop(first, last, body, 0)

    q_first = ((z + 6) % NZ) // 2

    def deltas(level, offset):
        base = ((q_first + 6 + offset) % 6) * 384
        choice = [[pick_ref[level, i * 4 + m] for m in range(4)] for i in range(4)]

        def body(i, carry):
            here = pl.ds(aligned(base + i * 32, 32), 32)
            modules = [
                weights[level][here, m * 128 : (m + 1) * 128].astype(F32) for m in range(4)
            ]
            totals = [None] * 4
            for p in range(4):
                gradient_p = grads[here, p * 128 : (p + 1) * 128]
                weight_p = choice[p][0] * modules[0]
                for m in range(1, 4):
                    weight_p = weight_p + choice[p][m] * modules[m]
                update = gradient_p / (jnp.abs(gradient_p) + adam_epsilon) + decay_rate * weight_p
                delta = (-inner_rate * update).astype(BF).astype(F32)
                for m in range(4):
                    term = choice[p][m] * delta
                    totals[m] = term if p == 0 else totals[m] + term
            for m in range(4):
                parts[level][here, m * 128 : (m + 1) * 128] = totals[m].astype(BF)
            return carry

        lax.fori_loop(0, 12, body, 0)

    rcopies = {}

    def pblock(level, zz, h):
        return parts[level].at[
            pl.ds(aligned(zz * BLOCK, 16), USED), h * 256 : (h + 1) * 256
        ]

    def ring(level, t):
        for h in range(2):
            for side in range(2):
                if t == 0 and h != side:
                    continue
                zz = (z + (6 - t if side == 0 else NZ - 6 + t)) % NZ
                src = pblock(level, zz, h)
                if (level, t - 1, side, h) in rcopies:
                    rcopies[level, t - 1, side, h].wait_recv()
                    held = recv.at[level, side, t - 1, h]
                    held[...] = (held[...].astype(F32) + src[...].astype(F32)).astype(BF)
                    src = held
                rcopies[level, t, side, h] = start(
                    src, recv.at[level, side, t, h], r_sem.at[level, t, side, h], to_z[side]
                )

    ocopies = []

    def finish(level):
        pieces = []
        for h in range(2):
            for side in range(2):
                rcopies[level, 5, side, h].wait_recv()
            total = (
                pblock(level, z, h)[...].astype(F32)
                + recv[level, 0, 5, h].astype(F32)
                + recv[level, 1, 5, h].astype(F32)
            ).astype(BF)
            pieces += [total[:, :128], total[:, 128:]]
        work[level] = (
            jnp.dot(perm_ref[...], jnp.concatenate(pieces, axis=0), preferred_element_type=F32)
            .astype(BF)
            .reshape(4, USED, 128)
        )
        for step in (1, 2, 3):
            other = (y_lo + step) % NYL
            ocopies.append(
                start(
                    work.at[level, other],
                    out_ref.at[level, y_lo],
                    o_sem.at[level, step - 1],
                    device(z, y_hi * NYL + other, x, core),
                )
            )
        out_ref[level, y_lo] = work[level, y_lo]

    z_first(0)
    routed[1].wait_recv()
    routed[2].wait_recv()
    b_y_send(0)
    b_x_send(0)

    @pl.when(x == 0)
    def _():
        own_rows.wait()

    @pl.when(x != 0)
    def _():
        routed[0].wait_recv()

    own = a_unit(x)
    a_right = start(own, own, ax_sem.at[0], to_x[0])
    a_left = start(own, own, ax_sem.at[1], to_x[1])
    a_right.wait_recv()
    passed = a_unit(x_left)
    a_far = start(passed, passed, ax_sem.at[2], to_x[0])
    y_wait("b", 0)
    b_y_send(1)
    b_x_send(1)
    b_x_send(2)
    a_left.wait_recv()
    a_far.wait_recv()
    a_y_send(0)
    z_first(1)
    z_step(0, 1)
    y_wait("b", 1)
    b_y_send(2)
    b_x_send(3)
    b_x_send(4)
    y_wait("a", 0)
    a_y_send(1)
    y_wait("b", 2)
    b_y_send(3)
    b_x_send(5)
    b_x_send(6)
    z_step(0, 2)
    y_wait("b", 3)
    b_x_send(7)
    core_send(0, b_slab(x))
    y_wait("a", 1)
    a_y_send(2)
    b_forward(0)
    b_forward(1)
    z_step(0, 3)
    y_wait("a", 2)
    a_y_send(3)
    b_forward(2)
    b_forward(3)
    z_step(0, 4)
    b_forward(4)
    b_forward(5)
    y_wait("a", 3)
    core_send(1, xs.at[core, pl.ds(0, 256), :])
    z_step(1, 1)
    b_forward(6)
    b_forward(7)
    z_step(0, 5)
    for n in range(8):
        xcopies[n, 1 - n % 2].wait_recv()
    core_send(2, b_slab(x_left))
    core_send(3, b_slab(x_right))
    for n in range(8):
        fcopies[n].wait_recv()
    core_send(4, b_slab(x_far))
    z_step(1, 2)
    z_last(0)
    for copy in scopies:
        copy.wait_recv()

    forward(0, 2)
    forward(2, 4)
    row_sums(0, act_ref, act_ref)
    sums_send(0, 0)
    z_step(1, 3)
    turn(1, 0, 9)
    mid_ref[0] = sums_wait(0, 0)
    sums_send(0, 1)
    turn(1, 9, 18)
    z_step(1, 4)
    squares = sums_wait(0, 1)
    make_hidden(squares)
    gradient(1, 0, 3)
    z_step(1, 5)
    gradient(1, 3, 6)
    z_last(1)

    deltas(1, 0)
    ring(1, 0)
    deltas(1, -1)
    deltas(1, 1)
    backward(0, 2)
    ring(1, 1)
    deltas(1, -2)
    deltas(1, 2)
    backward(2, 4)
    row_sums(1, back_ref, act_ref)
    sums_send(1, 0)
    ring(1, 2)
    deltas(1, 3)
    turn(0, 0, 9)
    mid_ref[1] = sums_wait(1, 0)
    sums_send(1, 1)
    ring(1, 3)
    turn(0, 9, 18)
    products = sums_wait(1, 1)
    make_dpre(products)
    gradient(0, 0, 3)
    ring(1, 4)
    gradient(0, 3, 6)
    deltas(0, 0)
    ring(1, 5)
    ring(0, 0)
    deltas(0, -1)
    deltas(0, 1)
    ring(0, 1)
    finish(1)
    deltas(0, -2)
    deltas(0, 2)
    ring(0, 2)
    deltas(0, 3)
    for t in (3, 4, 5):
        ring(0, t)
    finish(0)

    for copy in ocopies:
        copy.wait_recv()
    for copy in started:
        copy.wait_send()
    routed[1].wait_send()
    routed[2].wait_send()

    @pl.when(x != 0)
    def _():
        routed[0].wait_send()


VMEM = pl.BlockSpec(memory_space=pltpu.VMEM)
SMEM = pl.BlockSpec(memory_space=pltpu.SMEM)
DMA = pltpu.SemaphoreType.DMA


def fused(rows, weights, masks, picks):
    return pl.pallas_call(
        fused_kernel,
        out_shape=jax.ShapeDtypeStruct((2, 4, USED, 128), BF),
        in_specs=[VMEM, VMEM, VMEM, SMEM],
        out_specs=VMEM,
        scratch_shapes=[
            pltpu.VMEM((2, PLANE, WIDE), BF),
            pltpu.VMEM((2, WIDE, PLANE), BF),
            pltpu.VMEM((WIDE, 512), BF),
            pltpu.VMEM((WIDE, 512), BF),
            pltpu.VMEM((WIDE, 512), F32),
            pltpu.VMEM((WIDE, 512), BF),
            pltpu.VMEM((WIDE, 512), BF),
            pltpu.VMEM((PLANE, 128), F32),
            pltpu.VMEM((PLANE, 128), F32),
            pltpu.VMEM((PLANE, 128), F32),
            pltpu.VMEM((PLANE, 128), F32),
            pltpu.VMEM((PLANE, 512), BF),
            pltpu.VMEM((704, 704), BF),
            pltpu.VMEM((2, 4, USED, 128), BF),
            pltpu.VMEM((2, USED, 512), BF),
            pltpu.VMEM((2, 2, 6, 2, USED, 256), BF),
            pltpu.VMEM((2, 4, USED, 128), BF),
            pltpu.VMEM((2, 8, 128), F32),
            pltpu.VMEM((2, 8, 128), F32),
            pltpu.VMEM((2, 2, 8, 8, 128), F32),
            DMA((3, 2)),
            DMA((2, 3, 2)),
            DMA((2, 6, 2, 2, 2)),
            DMA((2, 6, 2, 2, 2)),
            DMA((3, 2)),
            DMA((4, 2, 2)),
            DMA((4, 2, 2)),
            DMA((8, 2, 2)),
            DMA((8, 2)),
            DMA((5, 2)),
            DMA((2, 2, 7, 2)),
            DMA((2, 3, 2)),
            DMA,
        ],
        compiler_params=pltpu.CompilerParams(
            collective_id=0, has_side_effects=True, vmem_limit_bytes=56 * 1024 * 1024
        ),
        name="fused",
    )(rows, weights, masks, picks)


def on_device(
    tokens,
    out_grad,
    doc_lengths,
    doc_paths,
    membership,
    up_master,
    down_master,
    up_moment,
    down_moment,
):
    path_count = lax.axis_size("path")
    row_count, width = tokens.shape
    module_count, owner_rows, owner_columns = up_master.shape
    capacity = row_count // path_count
    z, y_lo, y_hi, x, core = place()

    placing = placing_matrix(doc_lengths[0], doc_paths[0], row_count, path_count, capacity)
    rows_float = tokens.astype(F32)
    normed = (
        rows_float
        * lax.rsqrt(jnp.mean(rows_float * rows_float, axis=1, keepdims=True) + norm_epsilon)
    ).astype(BF)
    chosen = jnp.where(core == 0, normed, out_grad)
    half = jnp.where(y_hi == 0, chosen[:, : width // 2], chosen[:, width // 2 :])
    rows = jnp.dot(placing, half, preferred_element_type=F32).astype(BF)
    rows = jnp.concatenate(
        [
            jnp.pad(rows[:, k * USED : (k + 1) * USED], ((0, 0), (0, BLOCK - USED)))
            for k in range(NZ // 2)
        ],
        axis=1,
    )

    def blocks(master):
        flat = master.astype(BF).reshape(module_count * owner_rows, NYL, 128)
        return flat.transpose(1, 0, 2)

    weights_out = jnp.stack([blocks(up_master), blocks(down_master)])

    members = lax.dynamic_slice_in_dim(membership, z * NYL, NYL, 0)
    module_ids = jnp.arange(module_count, dtype=jnp.int32)
    picks = (members.T[:, :, None] == module_ids).astype(F32)
    masks = jnp.repeat(jnp.repeat(picks, capacity, axis=1), 128, axis=2)

    summed = fused(rows, weights_out, masks, picks.reshape(2, NYL * module_count))

    def update(master, moment, level):
        counts = jnp.sum((membership[:, level][None, :] == module_ids[:, None]).astype(F32), axis=1)
        total = (
            summed[level]
            .reshape(NYL, module_count, owner_rows, 128)
            .transpose(1, 2, 0, 3)
            .reshape(module_count, owner_rows, owner_columns)
        )
        return outer_update(master, moment, total.astype(F32), counts)

    new_up, new_up_moment = update(up_master, up_moment, 0)
    new_down, new_down_moment = update(down_master, down_moment, 1)
    return (new_up, new_down, new_up_moment, new_down_moment)


def solution(mesh):
    split = P(None, "path", "shard")
    rows = P("path", None)
    return jax.shard_map(
        on_device,
        mesh=mesh,
        in_specs=(rows, rows, rows, rows, P(), split, split, split, split),
        out_specs=(split, split, split, split),
        check_vma=False,
    )
```

time: 566 us -> 161 us (0.28); the launches traced: 559 us -> 160 us
  waiting for transfers between devices: 208 us -> 0 us
  blocking collectives: 194 us -> 0 us
  Pallas kernels: 0 us -> 146 us
  starting transfers between devices: 94.7 us -> 0 us
  local copies, waits for them, and re-layouts: 33.5 us -> 5.14 us
  matrix products: 17.6 us -> 0.42 us
    all_to_all x8 -> x0, waiting for transfers between devices: 208 us -> none  [the longest x4 117 us: ship(): lax.all_to_all(outgoing, 'path', split_axis=0, concat_axis=0, tiled=True)]
    pallas_call x0 -> x1, Pallas kernels: none -> 146 us  [fused(): pl.pallas_call(fused_kernel, out_shape=jax.ShapeDtypeStruct((2, 4, USED,...]
    all_to_all x2 -> x0, blocking collectives: 103 us -> none  [fetch(): lax.all_to_all(outgoing, 'path', split_axis=0, concat_axis=1, tiled=True)]
    all_to_all x8 -> x0, starting transfers between devices: 94.7 us -> none  [the longest x4 46 us: ship(): lax.all_to_all(outgoing, 'path', split_axis=0, concat_axis=0, tiled=True)]
    psum x2 -> x0, blocking collectives: 91.6 us -> none  [the longest x1 46.9 us: on_device(): squares = lax.psum(jnp.sum(activated * activated, axis=1), 'shard')]
    dot_general x10 -> x1, matrix products: 17.6 us -> 0.42 us  [on_device(): rows = jnp.dot(placing, half, preferred_element_type=F32).astype(BF)]
    squeeze x5 -> x0, local copies, waits for them, and re-layouts: 8.66 us -> none  [the longest x4 8.65 us: fetch(): halves.append(incoming[0])]
  transfers between devices with their start and end apart: 8 -> 0, of which waited for: 6 -> 0; matrix products, arithmetic and copies ran while one was open for 7% -> 0% of each run, Pallas kernels for 0% -> 0%
where the time goes in v2:
time: 161 us; the launch traced here: 160 us
  Pallas kernels  146 us (91%)
  other arithmetic  8.18 us (5%)
  local copies, waits for them, and re-layouts  5.14 us (3%)
    pallas_call x1, Pallas kernels, fused(): pl.pallas_call(fused_kernel, out_shape=jax.ShapeDtypeStruct((2, 4, USED,...  146 us

profile of v2, /device:TPU:56, one launch (start us, length us, event | category | flops | bytes accessed | tf_op | source)
XLA Modules:
  0.0 160.2 jit_solution(6633734144127510136)
XLA Ops:
  0.7 1.5 fusion
  2.2 0.3 fusion.2
  2.5 0.3 copy-done.7
  2.9 0.1 reduce
  3.3 0.6 reduce-window.19
  3.9 0.2 slice_reduce_fusion
  4.2 0.4 convolution_convert_fusion
  4.7 0.2 fusion.11
  5.0 0.3 copy-done.6
  5.3 1.0 concatenate.3.rows_ref
  6.6 0.7 reshape.102.mask_ref
  7.5 0.6 compare_convert_fusion.pick_ref
  8.5 0.8 pad_maximum_fusion.wsend_ref
  9.2 145.6 %fused.1 = bf16[2,4,176,128]{3,2,1,0:T(8,128)(2,1)} custom-call(bf16[192,1152]{1,0:T(8,128)(2,1)} %concatenate.3.rows_ref, bf16[2,4,176,128]{3,2,1,0:T(8,128)(2,1)} %pad_maximum_fusion.wsend_ref, f32[2,16,512]{2,1,0:T(8,128)} %reshape.102.mask_ref, f32[2,16]{1,0:T(2,128)} %compare_convert_fusion.pick_ref), custom_call_target="tpu_custom_call" | custom-call | tf_op jit(solution)/shard_map/fused/pallas_call | solution.py:663
  154.8 1.1 convert_negate_fusion
  155.9 0.1 copy.55
  156.0 0.1 reshape.105
  156.2 0.1 convert_reduce_fusion.1
  156.3 0.5 copy-done.3
  156.8 1.3 fusion.5
  158.1 0.1 copy.53
  158.2 0.1 reshape.104
  158.4 0.6 copy-done.4
  159.0 1.3 fusion.6
  (50 shorter events, 1.5 us)
Async XLA Ops:
  0.6 1.5 copy-start
  2.1 0.7 copy-start.7
  2.2 1.0 copy-start.8
  4.7 0.7 copy-start.6
  5.0 1.4 copy-start.5
  5.0 3.1 %copy-start.1 = (f32[4,44,512]{2,0,1:T(4,128)S(1)}, f32[4,44,512]{2,0,1:T(4,128)}, u32[]{:S(2)}) copy-start(f32[4,44,512]{2,0,1:T(4,128)} %param.15) | copy-start | bytes 1081348
  6.3 1.9 %copy-start.2 = (f32[4,44,512]{2,0,1:T(4,128)S(1)}, f32[4,44,512]{2,0,1:T(4,128)}, u32[]{:S(2)}) copy-start(f32[4,44,512]{2,0,1:T(4,128)} %param.14) | copy-start | bytes 1081348
  155.9 0.9 copy-start.3
  158.1 0.9 copy-start.4

commit v3 on v2

v3 whole, which is shorter than its diff:
```python
import functools

import jax
import jax.numpy as jnp
from jax import lax
from jax.experimental import pallas as pl
from jax.experimental.pallas import tpu as pltpu
from jax.sharding import PartitionSpec as P

MESH = pl.DeviceIdType.MESH
BF = jnp.bfloat16
F32 = jnp.float32

FF = 8192
NZ = 12
NYL = 4
NY = 8
NX = 4
UNIT = 16
HALF = 1152
WIDE = 2304
BLOCK = 192
USED = 176
PLANE = 768
PART = (96, 80)
OFFS = (0, -1, 1, -2, 2, -3, 3, -4)

norm_epsilon = 1e-06
hidden_epsilon = 1e-05
adam_epsilon = 0.001
inner_rate = 0.05
decay_rate = 0.1
outer_rate = 0.7
momentum_coef = 0.9
gelu_coef = 0.7978845608
cubic_coef = 0.044715


def gelu_pair(values):
    inner = gelu_coef * (values + cubic_coef * values * values * values)
    tangent = jnp.tanh(inner)
    activated = 0.5 * values * (1.0 + tangent)
    slopes = 0.5 * (1.0 + tangent) + 0.5 * values * (1.0 - tangent * tangent) * gelu_coef * (
        1.0 + 3.0 * cubic_coef * values * values
    )
    return (activated, slopes)


def row_slots(lengths, targets, row_count, path_count, capacity):
    ends = jnp.cumsum(lengths)
    row_ids = jnp.arange(row_count, dtype=jnp.int32)
    doc_of_row = jnp.sum((row_ids[:, None] >= ends[None, :]).astype(jnp.int32), axis=1)
    doc_hit = doc_of_row[:, None] == jnp.arange(lengths.shape[0], dtype=jnp.int32)[None, :]
    row_path = jnp.sum(jnp.where(doc_hit, targets[None, :], 0), axis=1)
    path_hit = (row_path[:, None] == jnp.arange(path_count, dtype=jnp.int32)[None, :]).astype(
        jnp.int32
    )
    ranks = jnp.sum((jnp.cumsum(path_hit, axis=0) - 1) * path_hit, axis=1)
    return jnp.where(ranks < capacity, row_path * capacity + ranks, -1)


def outer_update(master, moment, summed, counts):
    pseudo = -summed / jnp.maximum(counts, 1.0)[:, None, None]
    buffer = momentum_coef * moment.astype(jnp.float32) + pseudo
    return (master - outer_rate * (pseudo + momentum_coef * buffer), buffer.astype(jnp.bfloat16))


def place():
    path = lax.axis_index("path")
    shard = lax.axis_index("shard")
    return path // NYL, path % NYL, shard // 8, (shard // 2) % NX, shard % 2


def device(z, y, x, core):
    return (z * NYL + y % NYL, ((y // NYL) * NX + x) * 2 + core)


def aligned(value, multiple):
    return pl.multiple_of(value, multiple)


def signal(to):
    pl.semaphore_signal(
        pltpu.get_barrier_semaphore(), inc=1, device_id=to, device_id_type=MESH
    )


def fused_kernel(
    tokens,
    out_grad,
    slots_ref,
    up_master,
    down_master,
    member_ref,
    up_sums,
    down_sums,
    mask_ref,
    total_ref,
    padded,
    chosen_ref,
    blocks_ref,
    wsend_ref,
    landed,
    back_perm,
    xs,
    xt,
    up_w,
    down_w,
    grads,
    up_p,
    down_p,
    act_ref,
    slope_ref,
    back_ref,
    scale_ref,
    spread_ref,
    perm_ref,
    wrecv,
    recv,
    work,
    sums_ref,
    mid_ref,
    slots,
    a_sem,
    e_sem,
    z_sem,
    r_sem,
    ax_sem,
    ay_sem,
    by_sem,
    bx_sem,
    f_sem,
    s_sem,
    t_sem,
    o_sem,
    l_sem,
):
    z, y_lo, y_hi, x, core = place()
    y = y_hi * NYL + y_lo
    c = x * 2 + core
    weights = (up_w, down_w)
    masters = (up_master, down_master)
    outputs = (up_sums, down_sums)
    parts = (up_p, down_p)

    def remote(src, dst, sems, to):
        return pltpu.make_async_remote_copy(
            src_ref=src,
            dst_ref=dst,
            send_sem=sems.at[0],
            recv_sem=sems.at[1],
            device_id=to,
            device_id_type=MESH,
        )

    started = []

    def start(src, dst, sems, to):
        copy = remote(src, dst, sems, to)
        copy.start()
        started.append(copy)
        return copy

    x_right, x_left, x_far = (x + 1) % NX, (x + 3) % NX, (x + 2) % NX
    to_x = (device(z, y, x_right, core), device(z, y, x_left, core))
    to_y = (device(z, (y + 1) % NY, x, core), device(z, (y + 7) % NY, x, core))
    to_z = (device((z + 1) % NZ, y, x, core), device((z + 11) % NZ, y, x, core))
    to_core = device(z, y, x, 1 - core)
    all_y = [device(z, (y + s) % NY, x, core) for s in range(1, NY)]
    all_c = [device(z, y, ((c + s) % 8) // 2, (c + s) % 2) for s in range(1, 8)]

    for to in all_y + all_c:
        signal(to)
    for to in to_z:
        signal(to)
    hops = [
        jnp.where(x == 0, a, jnp.where(x == 1, b, jnp.where(x == 2, c_, d)))
        for a, b, c_, d in ((0, 1, 2, 6), (5, 4, 3, 9), (7, 8, 11, 10))
    ]
    signal(device((z + NZ - jnp.where(x == 0, 6, hops[0])) % NZ, y, x, core))
    for j in (1, 2):
        signal(device((z + NZ - hops[j]) % NZ, y, x, core))
    for level in range(2):
        for other in range(4):
            for m in range(4):
                wsend_ref[level, other, m * 48 + 32 : m * 48 + 48, :] = jnp.zeros((16, 128), BF)
    for level in range(2):
        for m in range(4):
            values = masters[level][:, m, :].astype(BF)
            for other in range(4):
                wsend_ref[level, other, m * 48 : m * 48 + 44, :] = values[
                    :, other * 128 : (other + 1) * 128
                ]
    rows_float = tokens[...].astype(F32)
    normed = (
        rows_float
        * lax.rsqrt(jnp.mean(rows_float * rows_float, axis=1, keepdims=True) + norm_epsilon)
    ).astype(BF)
    chosen_ref[...] = jnp.where(core == 0, normed, out_grad[...])
    blocks_ref[...] = jnp.zeros_like(blocks_ref)
    for n in range(NZ // 2):
        low = chosen_ref[:, n * USED : (n + 1) * USED]
        high = chosen_ref[:, (n + 6) * USED : (n + 7) * USED]
        blocks_ref[:, n * BLOCK : n * BLOCK + USED] = jnp.where(y_hi == 0, low, high)
    placing = (lax.broadcasted_iota(jnp.int32, (192, 192), 0) == slots_ref[...]).astype(F32)
    padded[...] = jnp.dot(
        placing.astype(BF), blocks_ref[...], preferred_element_type=F32
    ).astype(BF)
    pl.semaphore_wait(pltpu.get_barrier_semaphore(), 19)

    half_cols = pl.ds(aligned(y_hi * HALF, 128), HALF)

    def trade_columns(level):
        copies = []
        for step in (1, 2, 3):
            other = (y_lo + step) % NYL
            copies.append(
                start(
                    wsend_ref.at[level, other],
                    wrecv.at[level, y_lo],
                    e_sem.at[level, step - 1],
                    device(z, y_hi * NYL + other, x, core),
                )
            )
        wrecv[level, y_lo] = wsend_ref[level, y_lo]
        return copies

    trades = [trade_columns(0)]
    b_row = 256 + (x * NYL + y_lo) * 32
    landing = [
        xs.at[core, pl.ds(aligned((y_lo * NX + x) * UNIT, 16), UNIT), half_cols],
        xs.at[core, pl.ds(aligned(b_row, 16), UNIT), half_cols],
        xs.at[core, pl.ds(aligned(b_row + UNIT, 16), UNIT), half_cols],
    ]
    routed = []
    for j in range(3):
        target = (z + hops[j]) % NZ
        routed.append(
            remote(
                padded.at[pl.ds(aligned(target * UNIT, 16), UNIT), :],
                landing[j],
                a_sem.at[j],
                device(target, y, x, core),
            )
        )
    own_rows = pltpu.make_async_copy(
        padded.at[pl.ds(aligned(z * UNIT, 16), UNIT), :], landing[0], l_sem
    )
    routed[1].start()
    routed[2].start()

    @pl.when(x == 0)
    def _():
        own_rows.start()

    @pl.when(x != 0)
    def _():
        routed[0].start()

    for level in range(2):
        for zz in range(NZ):
            weights[level][zz * BLOCK + USED : (zz + 1) * BLOCK, :] = jnp.zeros(
                (BLOCK - USED, 512), BF
            )
    sums_ref[...] = jnp.zeros_like(sums_ref)
    choice = [
        [
            [jnp.where(member_ref[level, z * NYL + i] == m, 1.0, 0.0) for m in range(4)]
            for i in range(4)
        ]
        for level in range(2)
    ]
    path_of_row = lax.broadcasted_iota(jnp.int32, (16, 128), 0) // 4
    for level in range(2):
        for m in range(4):
            mask_ref[level, :, m * 128 : (m + 1) * 128] = sum(
                jnp.where(path_of_row == i, choice[level][i][m], 0.0) for i in range(4)
            )

    def fill_perm(i, carry):
        here = pl.ds(aligned(i * 16, 16), 16)
        a = lax.broadcasted_iota(jnp.int32, (16, 1), 0) + i * 16
        b = lax.broadcasted_iota(jnp.int32, (16, 768), 1)
        first = sum((a >= 176 * n).astype(jnp.int32) for n in (1, 2, 3))
        rest = a - 176 * first
        second = sum((rest >= 44 * n).astype(jnp.int32) for n in (1, 2, 3))
        to_b = second * 192 + first * 48 + rest - 44 * second
        perm_ref[here, :] = jnp.where(b == to_b, 1.0, 0.0).astype(BF)
        return carry

    def fill_back(i, carry):
        here = pl.ds(aligned(i * 16, 16), 16)
        b = lax.broadcasted_iota(jnp.int32, (16, 1), 0) + i * 16
        a = lax.broadcasted_iota(jnp.int32, (16, 704), 1)
        first = sum((b >= 192 * n).astype(jnp.int32) for n in (1, 2, 3))
        rest = b - 192 * first
        second = sum((rest >= 48 * n).astype(jnp.int32) for n in (1, 2, 3))
        row = rest - 48 * second
        to_a = jnp.where(row < 44, second * 176 + first * 44 + row, -1)
        back_perm[here, :] = jnp.where(a == to_a, 1.0, 0.0).astype(BF)
        return carry

    def constants():
        lax.fori_loop(0, 48, fill_back, 0)

    lax.fori_loop(0, 44, fill_perm, 0)

    zcopies = {}

    def wblock(level, zz, h):
        return weights[level].at[
            pl.ds(aligned(zz * BLOCK, 16), USED), h * 256 : (h + 1) * 256
        ]

    def z_send(level, t, side, h):
        zz = (z + NZ + (-t if side == 0 else t)) % NZ
        dst = wblock(level, zz, h)
        zcopies[level, t, side, h] = start(dst, dst, z_sem.at[level, t, side, h], to_z[side])

    def z_first(level):
        for copy in trades[level]:
            copy.wait_recv()
        pieces = wrecv[level].reshape(4 * BLOCK, 128)
        for m in range(4):
            weights[level][pl.ds(aligned(z * BLOCK, 16), USED), m * 128 : (m + 1) * 128] = jnp.dot(
                perm_ref[m * USED : (m + 1) * USED, :], pieces, preferred_element_type=F32
            ).astype(BF)
        for h in range(2):
            for side in range(2):
                z_send(level, 0, side, h)

    def z_got(level, t, side, h):
        zcopies[level, t, side, h].wait_recv()
        if t < 4 or (t == 4 and h == side):
            z_send(level, t + 1, side, h)

    def a_unit(xx):
        return a_part(xx, y)

    def cols_of(yy):
        return pl.ds(aligned((yy // NYL) * HALF, 128), HALF)

    def a_part(xx, yy):
        return xs.at[
            core, pl.ds(aligned(((yy % NYL) * NX + xx) * UNIT, 16), UNIT), cols_of(yy)
        ]

    def b_chunk(xx, yy):
        return xs.at[
            core, pl.ds(aligned(256 + (xx * NYL + yy % NYL) * 32, 16), 32), cols_of(yy)
        ]

    def b_slab(xx):
        return xs.at[core, pl.ds(aligned(256 + xx * 128, 16), 128), :]

    ycopies = {}

    def y_send(name, block, sems, t, side):
        ref = block((y + NY + (-t if side == 0 else t)) % NY)
        ycopies[name, t, side] = start(ref, ref, sems.at[t, side], to_y[side])

    def b_y_send(t, side):
        y_send("b", lambda yy: b_chunk(x, yy), by_sem, t, side)

    def a_y_send(k, t, side):
        y_send(k, lambda yy: a_part(lanes_a[k], yy), ay_sem.at[k], t, side)

    def onward(t, side):
        return t < 3 and (side == 0 or t < 2)

    lanes_a = (x, x_left, x_right, x_far)
    xcopies = {}
    fcopies = {}
    acopies = {}
    scopies = []

    def b_x_send(n):
        ref = b_chunk(x, (y + NY + OFFS[n]) % NY)
        for side in range(2):
            xcopies[n, side] = start(ref, ref, bx_sem.at[n, side], to_x[side])

    def core_send(index):
        ref = xs.at[core, pl.ds(0, 256), :] if index == 1 else b_slab((x, x, x_left, x_right, x_far)[index])
        scopies.append(start(ref, ref, s_sem.at[len(scopies)], to_core))

    def rows_got():
        routed[1].wait_recv()
        routed[2].wait_recv()
        b_y_send(0, 0)
        b_y_send(0, 1)

        @pl.when(x == 0)
        def _():
            own_rows.wait()

        @pl.when(x != 0)
        def _():
            routed[0].wait_recv()

        own = a_unit(x)
        for side in range(2):
            acopies[side] = start(own, own, ax_sem.at[side], to_x[side])
        a_y_send(0, 0, 0)
        a_y_send(0, 0, 1)
        b_x_send(0)

    def a_x_got(i):
        acopies[i].wait_recv()
        if i == 0:
            passed = a_unit(x_left)
            acopies[2] = start(passed, passed, ax_sem.at[2], to_x[0])
        a_y_send(i + 1, 0, 0)
        a_y_send(i + 1, 0, 1)

    def b_y_got(t, side):
        ycopies["b", t, side].wait_recv()
        if onward(t, side):
            b_y_send(t + 1, side)
        b_x_send(2 * t + 1 + side)

    def a_y_got(k, t, side):
        ycopies[k, t, side].wait_recv()
        if onward(t, side):
            a_y_send(k, t + 1, side)

    def b_x_got(n, side):
        xcopies[n, side].wait_recv()
        if n % 2 == side:
            ref = b_chunk((x_left, x_right)[side], (y + NY + OFFS[n]) % NY)
            fcopies[n] = start(ref, ref, f_sem.at[n], to_x[side])

    def f_got(n):
        fcopies[n].wait_recv()

    tcopies = {}

    def sums_send(which, stage):
        src = (sums_ref, mid_ref)[stage].at[which]
        mine = (y, c)[stage]
        tcopies[which, stage] = [
            start(src, slots.at[which, stage, mine], t_sem.at[which, stage, s], to)
            for s, to in enumerate((all_y, all_c)[stage])
        ]
        slots[which, stage, mine] = src[...]

    def sums_wait(which, stage):
        for copy in tcopies[which, stage]:
            copy.wait_recv()
        total = slots[which, stage, 0]
        for i in range(1, 8):
            total += slots[which, stage, i]
        return total

    def picked(product, level):
        masked = product.reshape(12, 16, 512) * mask_ref[level][None]
        total = masked[:, :, :128]
        for m in range(1, 4):
            total = total + masked[:, :, m * 128 : (m + 1) * 128]
        return total.reshape(BLOCK, 128)

    def forward(first, last):
        def body(i, carry):
            here = pl.ds(aligned(i * BLOCK, 16), BLOCK)
            pre = picked(jnp.dot(xs[0, here, :], up_w[...], preferred_element_type=F32), 0)
            act_ref[here, :], slope_ref[here, :] = gelu_pair(pre)
            return carry

        lax.fori_loop(first, last, body, 0)

    def backward(first, last):
        def body(i, carry):
            here = pl.ds(aligned(i * BLOCK, 16), BLOCK)
            back_ref[here, :] = picked(
                jnp.dot(xs[1, here, :], down_w[...], preferred_element_type=F32), 1
            )
            return carry

        lax.fori_loop(first, last, body, 0)

    def row_sums(which, left, right):
        for k in range(6):
            here = slice(k * 128, (k + 1) * 128)
            sums_ref[which, k : k + 1, :] = jnp.sum(
                (left[here, :] * right[here, :]).T, axis=0, keepdims=True
            )

    def column(row):
        return jnp.broadcast_to(row, (128, 128)).T

    def store_spread(k, values):
        here = slice(k * 128, (k + 1) * 128)
        path = (lax.broadcasted_iota(jnp.int32, (128, 128), 0) // 4) % 4
        for i in range(4):
            spread_ref[here, i * 128 : (i + 1) * 128] = jnp.where(path == i, values, 0.0).astype(BF)

    def make_hidden(total):
        scale_row = jnp.sqrt(total / FF + hidden_epsilon)
        for k in range(6):
            here = slice(k * 128, (k + 1) * 128)
            scale = column(scale_row[k : k + 1, :])
            scale_ref[here, :] = scale
            hidden = act_ref[here, :] / scale
            act_ref[here, :] = hidden
            store_spread(k, hidden)

    def make_dpre(total):
        mix_row = total / FF
        for k in range(6):
            here = slice(k * 128, (k + 1) * 128)
            mixing = column(mix_row[k : k + 1, :])
            hidden = act_ref[here, :]
            store_spread(
                k,
                (back_ref[here, :] - hidden * mixing) / scale_ref[here, :] * slope_ref[here, :],
            )

    def turn(which, first, last):
        def body(i, carry):
            here = pl.ds(aligned(i * 128, 128), 128)
            xt[which, here, :] = xs[which, :, here].T
            return carry

        lax.fori_loop(first, last, body, 0)

    def gradient(which, first, last):
        def body(i, carry):
            here = pl.ds(aligned(i * 384, 128), 384)
            grads[here, :] = jnp.dot(
                xt[which, here, :], spread_ref[...], preferred_element_type=F32
            )
            return carry

        lax.fori_loop(first, last, body, 0)

    q_first = ((z + 6) % NZ) // 2

    def deltas(level, offset):
        base = ((q_first + 6 + offset) % 6) * 384
        chosen = choice[level]

        def body(i, carry):
            here = pl.ds(aligned(base + i * 32, 32), 32)
            modules = [
                weights[level][here, m * 128 : (m + 1) * 128].astype(F32) for m in range(4)
            ]
            totals = [None] * 4
            for p in range(4):
                gradient_p = grads[here, p * 128 : (p + 1) * 128]
                weight_p = chosen[p][0] * modules[0]
                for m in range(1, 4):
                    weight_p = weight_p + chosen[p][m] * modules[m]
                size = jnp.abs(gradient_p) + adam_epsilon
                inverse = pl.reciprocal(size, approx=True)
                inverse = inverse * (2.0 - size * inverse)
                update = gradient_p * inverse + decay_rate * weight_p
                delta = (-inner_rate * update).astype(BF).astype(F32)
                for m in range(4):
                    term = chosen[p][m] * delta
                    totals[m] = term if p == 0 else totals[m] + term
            for m in range(4):
                parts[level][here, m * 128 : (m + 1) * 128] = totals[m].astype(BF)
            return carry

        lax.fori_loop(0, 12, body, 0)

    rcopies = {}

    def pblock(level, zz, h):
        return parts[level].at[
            pl.ds(aligned(zz * BLOCK + 96 * h, 16), PART[h]), :
        ]

    def held_part(level, side, t, h):
        return recv.at[level, side, t, 96 * h : 96 * h + PART[h], :]

    def ring_part(level, t, side, h):
        zz = (z + (6 - t if side == 0 else NZ - 6 + t)) % NZ
        src = pblock(level, zz, h)
        if (level, t - 1, side, h) in rcopies:
            rcopies[level, t - 1, side, h].wait_recv()
            held = held_part(level, side, t - 1, h)
            held[...] = (held[...].astype(F32) + src[...].astype(F32)).astype(BF)
            src = held
        rcopies[level, t, side, h] = start(
            src, held_part(level, side, t, h), r_sem.at[level, t, side, h], to_z[side]
        )

    ocopies = {}

    def finish(level):
        totals = []
        for h in range(2):
            for side in range(2):
                rcopies[level, 5, side, h].wait_recv()
            totals.append(
                pblock(level, z, h)[...].astype(F32)
                + held_part(level, 0, 5, h)[...].astype(F32)
                + held_part(level, 1, 5, h)[...].astype(F32)
            )
        total = jnp.concatenate(totals, axis=0).astype(BF)
        pieces = [total[:, m * 128 : (m + 1) * 128] for m in range(4)]
        work[level] = (
            jnp.dot(back_perm[...], jnp.concatenate(pieces, axis=0), preferred_element_type=F32)
            .astype(BF)
            .reshape(4, BLOCK, 128)
        )
        for step in (1, 2, 3):
            other = (y_lo + step) % NYL
            ocopies[level, step] = start(
                work.at[level, other],
                landed.at[level, y_lo],
                o_sem.at[level, step - 1],
                device(z, y_hi * NYL + other, x, core),
            )
        landed[level, y_lo] = work[level, y_lo]

    def outer(level):
        for step in (1, 2, 3):
            ocopies[level, step].wait_recv()
        for m in range(4):
            total_ref[:, m, :] = jnp.concatenate(
                [landed[level, n, m * 48 : m * 48 + 44, :].astype(F32) for n in range(4)], axis=1
            )
        outputs[level][...] = total_ref[...].astype(BF)

    z_first(0)
    constants()
    rows_got()
    z_got(0, 0, 0, 0)
    z_got(0, 0, 1, 0)
    a_x_got(0)
    a_x_got(1)
    b_y_got(0, 0)
    z_got(0, 0, 0, 1)
    b_y_got(0, 1)
    z_got(0, 0, 1, 1)
    a_y_got(0, 0, 0)
    a_y_got(0, 0, 1)
    b_x_got(0, 0)
    b_x_got(0, 1)
    a_x_got(2)
    a_y_got(1, 0, 0)
    z_got(0, 1, 0, 0)
    a_y_got(1, 0, 1)
    z_got(0, 1, 1, 0)
    a_y_got(2, 0, 0)
    a_y_got(2, 0, 1)
    b_x_got(1, 0)
    b_x_got(1, 1)
    z_got(0, 1, 0, 1)
    b_y_got(1, 0)
    trades.append(trade_columns(1))
    b_y_got(1, 1)
    z_got(0, 1, 1, 1)
    b_x_got(2, 0)
    a_y_got(0, 1, 0)
    b_x_got(2, 1)
    a_y_got(0, 1, 1)
    a_y_got(3, 0, 0)
    a_y_got(3, 0, 1)
    z_got(0, 2, 0, 0)
    f_got(0)
    a_y_got(1, 1, 0)
    a_y_got(1, 1, 1)
    z_got(0, 2, 1, 0)
    f_got(1)
    a_y_got(2, 1, 0)
    a_y_got(2, 1, 1)
    b_x_got(3, 0)
    z_got(0, 2, 0, 1)
    b_x_got(3, 1)
    b_y_got(2, 0)
    z_got(0, 2, 1, 1)
    b_x_got(4, 0)
    b_x_got(4, 1)
    z_got(0, 3, 0, 0)
    f_got(2)
    z_got(0, 3, 1, 0)
    f_got(3)
    z_got(0, 3, 0, 1)
    b_x_got(5, 0)
    b_y_got(2, 1)
    z_first(1)
    z_got(0, 3, 1, 1)
    a_y_got(0, 2, 0)
    a_y_got(0, 2, 1)
    b_x_got(5, 1)
    a_y_got(3, 1, 0)
    f_got(4)
    a_y_got(3, 1, 1)
    z_got(0, 4, 0, 0)
    a_y_got(1, 2, 0)
    a_y_got(1, 2, 1)
    z_got(0, 4, 1, 0)
    a_y_got(2, 2, 0)
    a_y_got(2, 2, 1)
    b_x_got(6, 0)
    b_x_got(6, 1)
    z_got(0, 4, 0, 1)
    b_y_got(3, 0)
    core_send(0)
    a_y_got(0, 3, 0)
    z_got(1, 0, 1, 0)
    a_y_got(3, 2, 1)
    f_got(5)
    z_got(1, 0, 0, 0)
    a_y_got(3, 2, 0)
    a_y_got(1, 3, 0)
    z_got(1, 0, 1, 1)
    f_got(6)
    z_got(1, 0, 0, 1)
    a_y_got(2, 3, 0)
    scopies[0].wait_recv()
    b_x_got(7, 1)
    core_send(3)
    b_x_got(7, 0)
    core_send(2)
    z_got(0, 4, 1, 1)
    a_y_got(3, 3, 0)
    core_send(1)
    z_got(0, 5, 0, 0)
    z_got(1, 1, 1, 0)
    scopies[3].wait_recv()
    z_got(1, 1, 0, 0)
    f_got(7)
    core_send(4)
    scopies[2].wait_recv()
    z_got(1, 1, 1, 1)
    z_got(1, 1, 0, 1)
    z_got(0, 5, 1, 1)
    scopies[1].wait_recv()
    scopies[4].wait_recv()
    forward(0, 2)
    z_got(1, 2, 0, 0)
    z_got(1, 2, 1, 0)
    z_got(1, 2, 0, 1)
    forward(2, 4)
    z_got(1, 2, 1, 1)
    row_sums(0, act_ref, act_ref)
    sums_send(0, 0)
    turn(1, 0, 6)
    z_got(1, 3, 0, 0)
    z_got(1, 3, 1, 0)
    turn(1, 6, 12)
    turn(1, 12, 18)
    z_got(1, 3, 0, 1)
    z_got(1, 3, 1, 1)
    mid_ref[0] = sums_wait(0, 0)
    sums_send(0, 1)
    z_got(1, 4, 0, 0)
    z_got(1, 4, 1, 0)
    z_got(1, 4, 0, 1)
    z_got(1, 4, 1, 1)
    make_hidden(sums_wait(0, 1))
    gradient(1, 0, 2)
    z_got(1, 5, 0, 0)
    gradient(1, 2, 4)
    gradient(1, 4, 6)
    z_got(1, 5, 1, 1)
    deltas(1, 0)
    ring_part(1, 0, 0, 0)
    ring_part(1, 0, 1, 1)
    deltas(1, -1)
    deltas(1, 1)
    ring_part(1, 1, 1, 0)
    ring_part(1, 1, 0, 1)
    backward(0, 2)
    backward(2, 4)
    ring_part(1, 1, 1, 1)
    ring_part(1, 1, 0, 0)
    ring_part(1, 2, 0, 1)
    ring_part(1, 2, 1, 0)
    row_sums(1, back_ref, act_ref)
    sums_send(1, 0)
    deltas(1, -2)
    deltas(1, 2)
    ring_part(1, 2, 1, 1)
    deltas(1, 3)
    ring_part(1, 2, 0, 0)
    turn(0, 0, 6)
    mid_ref[1] = sums_wait(1, 0)
    sums_send(1, 1)
    ring_part(1, 3, 1, 0)
    ring_part(1, 3, 0, 1)
    turn(0, 6, 12)
    ring_part(1, 3, 1, 1)
    turn(0, 12, 18)
    ring_part(1, 3, 0, 0)
    make_dpre(sums_wait(1, 1))
    gradient(0, 0, 2)
    ring_part(1, 4, 1, 0)
    ring_part(1, 4, 0, 1)
    ring_part(1, 4, 1, 1)
    gradient(0, 2, 4)
    ring_part(1, 4, 0, 0)
    gradient(0, 4, 6)
    deltas(0, 0)
    ring_part(0, 0, 0, 0)
    ring_part(0, 0, 1, 1)
    ring_part(1, 5, 1, 0)
    ring_part(1, 5, 0, 1)
    deltas(0, -1)
    deltas(0, 1)
    ring_part(1, 5, 1, 1)
    ring_part(1, 5, 0, 0)
    ring_part(0, 1, 1, 0)
    ring_part(0, 1, 0, 1)
    deltas(0, -2)
    ring_part(0, 1, 1, 1)
    ring_part(0, 1, 0, 0)
    deltas(0, 2)
    deltas(0, 3)
    finish(1)
    ring_part(0, 2, 1, 0)
    ring_part(0, 2, 0, 1)
    ring_part(0, 2, 1, 1)
    ring_part(0, 2, 0, 0)
    ring_part(0, 3, 1, 0)
    ring_part(0, 3, 0, 1)
    outer(1)
    ring_part(0, 3, 1, 1)
    ring_part(0, 3, 0, 0)
    ring_part(0, 4, 1, 0)
    ring_part(0, 4, 0, 1)
    ring_part(0, 4, 1, 1)
    ring_part(0, 4, 0, 0)
    ring_part(0, 5, 1, 0)
    ring_part(0, 5, 0, 1)
    ring_part(0, 5, 1, 1)
    ring_part(0, 5, 0, 0)
    finish(0)
    outer(0)

    for copy in started:
        copy.wait_send()
    routed[1].wait_send()
    routed[2].wait_send()

    @pl.when(x != 0)
    def _():
        routed[0].wait_send()


VMEM = pl.BlockSpec(memory_space=pltpu.VMEM)
SMEM = pl.BlockSpec(memory_space=pltpu.SMEM)
DMA = pltpu.SemaphoreType.DMA


def fused(tokens, out_grad, slots, masters, members):
    shape = masters[0].shape
    sums = jax.ShapeDtypeStruct(shape, BF)
    return pl.pallas_call(
        fused_kernel,
        out_shape=(sums, sums),
        in_specs=[VMEM, VMEM, VMEM, VMEM, VMEM, SMEM],
        out_specs=(VMEM, VMEM),
        scratch_shapes=[
            pltpu.VMEM((2, 16, 512), F32),
            pltpu.VMEM((44, 4, 512), F32),
            pltpu.VMEM((192, HALF), BF),
            pltpu.VMEM((192, 2112), BF),
            pltpu.VMEM((192, HALF), BF),
            pltpu.VMEM((2, 4, BLOCK, 128), BF),
            pltpu.VMEM((2, 4, BLOCK, 128), BF),
            pltpu.VMEM((768, 704), BF),
            pltpu.VMEM((2, PLANE, WIDE), BF),
            pltpu.VMEM((2, WIDE, PLANE), BF),
            pltpu.VMEM((WIDE, 512), BF),
            pltpu.VMEM((WIDE, 512), BF),
            pltpu.VMEM((WIDE, 512), F32),
            pltpu.VMEM((WIDE, 512), BF),
            pltpu.VMEM((WIDE, 512), BF),
            pltpu.VMEM((PLANE, 128), F32),
            pltpu.VMEM((PLANE, 128), F32),
            pltpu.VMEM((PLANE, 128), F32),
            pltpu.VMEM((PLANE, 128), F32),
            pltpu.VMEM((PLANE, 512), BF),
            pltpu.VMEM((704, 768), BF),
            pltpu.VMEM((2, 4, BLOCK, 128), BF),
            pltpu.VMEM((2, 2, 6, USED, 512), BF),
            pltpu.VMEM((2, 4, BLOCK, 128), BF),
            pltpu.VMEM((2, 8, 128), F32),
            pltpu.VMEM((2, 8, 128), F32),
            pltpu.VMEM((2, 2, 8, 8, 128), F32),
            DMA((3, 2)),
            DMA((2, 3, 2)),
            DMA((2, 6, 2, 2, 2)),
            DMA((2, 6, 2, 2, 2)),
            DMA((3, 2)),
            DMA((4, 4, 2, 2)),
            DMA((4, 2, 2)),
            DMA((8, 2, 2)),
            DMA((8, 2)),
            DMA((5, 2)),
            DMA((2, 2, 7, 2)),
            DMA((2, 3, 2)),
            DMA,
        ],
        compiler_params=pltpu.CompilerParams(
            collective_id=0, has_side_effects=True, vmem_limit_bytes=56 * 1024 * 1024
        ),
        name="fused",
    )(tokens, out_grad, slots, *masters, members)


def on_device(
    tokens,
    out_grad,
    doc_lengths,
    doc_paths,
    membership,
    up_master,
    down_master,
    up_moment,
    down_moment,
):
    path_count = lax.axis_size("path")
    row_count = tokens.shape[0]
    capacity = row_count // path_count

    slots = row_slots(doc_lengths[0], doc_paths[0], row_count, path_count, capacity)

    def turned(array):
        return array.transpose(1, 0, 2)

    sums = fused(
        tokens, out_grad, slots[None, :], (turned(up_master), turned(down_master)), membership.T
    )
    module_ids = jnp.arange(up_master.shape[0], dtype=jnp.int32)

    def update(master, moment, level):
        counts = jnp.sum((membership[:, level][None, :] == module_ids[:, None]).astype(F32), axis=1)
        return outer_update(master, moment, turned(sums[level]).astype(F32), counts)

    new_up, new_up_moment = update(up_master, up_moment, 0)
    new_down, new_down_moment = update(down_master, down_moment, 1)
    return (new_up, new_down, new_up_moment, new_down_moment)


def solution(mesh):
    split = P(None, "path", "shard")
    rows = P("path", None)
    return jax.shard_map(
        on_device,
        mesh=mesh,
        in_specs=(rows, rows, rows, rows, P(), split, split, split, split),
        out_specs=(split, split, split, split),
        check_vma=False,
    )
```

time: 161 us -> 148 us (0.919)
  Pallas kernels: 146 us -> 140 us
  other arithmetic: 8.18 us -> 5.01 us
  local copies, waits for them, and re-layouts: 5.14 us -> 2.18 us
    pallas_call x1, Pallas kernels: 146 us -> 140 us  [fused(): pl.pallas_call(fused_kernel, out_shape=(sums, sums), in_specs=[VMEM, VMEM...]
where the time goes in v3:
time: 148 us
  Pallas kernels  140 us (95%)
  other arithmetic  5.01 us (3%)
  local copies, waits for them, and re-layouts  2.18 us (1%)
    pallas_call x1, Pallas kernels, fused(): pl.pallas_call(fused_kernel, out_shape=(sums, sums), in_specs=[VMEM, VMEM...  140 us
    convert_element_type x2, other arithmetic, outer_update(): buffer.astype(jnp.bfloat16)  3.2 us

profile of v3, /device:TPU:56, one launch (start us, length us, event | category | flops | bytes accessed | tf_op | source)
XLA Modules:
  0.0 147.7 jit_solution(2925827022688799694)
XLA Ops:
  0.6 0.0 copy-start.5
  0.6 0.7 copy-done.5
  1.3 0.1 convert_reduce_fusion.1
  1.5 0.6 copy-done.6
  2.1 0.1 copy.17
  2.2 0.1 reduce
  2.4 0.1 convert_reduce_fusion
  2.4 0.6 copy-done.7
  3.0 0.1 select_reduce_fusion
  3.1 0.6 reduce-window.19
  3.7 0.2 slice_reduce_fusion
  4.0 0.1 bitcast_bitcast_fusion
  4.1 0.6 compare_select_fusion
  4.7 139.7 %fused.1 = (bf16[44,4,512]{2,1,0:T(4,128)(2,1)}, bf16[44,4,512]{2,1,0:T(4,128)(2,1)}) custom-call(bf16[192,2112]{1,0:T(8,128)(2,1)} %tokens.1, bf16[192,2112]{1,0:T(8,128)(2,1)} %out_grad.1, s32[1,192]{1,0:T(1,128)} %bitcast.46, f32[44,4,512]{2,1,0:T(4,128)} %bitcast.44, f32[44,4,512]{2,1,0:T(4,128)} %bitcast.45, s32[2,48]{1,0:T(2,128)} %bitcast.47), custom_call_target="tpu_custom_call" | custom-call | tf_op jit(solution)/shard_map/fused/pallas_call | solution.py:852
  144.4 0.0 copy-done
  144.4 0.0 copy-done.2
  144.4 0.0 copy-start.1
  144.4 0.0 copy-start.3
  144.4 0.0 copy-start.4
  144.5 2.1 %fusion.5 = (bf16[4,44,512]{2,0,1:T(4,128)(2,1)}, f32[4,44,512]{2,0,1:T(4,128)}) fusion(bf16[4,44,512]{2,0,1:T(4,128)(2,1)S(1)} %copy-done.2, f32[4]{0:T(128)S(1)} %broadcast_maximum_fusion.1, bf16[44,4,512]{2,1,0:T(4,128)(2,1)} %get-tuple-element.6, f32[4,44,512]{2,0,1:T(4,128)S(1)} %copy-done), kind=kLoop, calls=%fused_computation.10 | loop fusion | flops 991232 | bytes 1261584 | tf_op jit(solution)/shard_map/convert_element_type | solution.py:65
  146.5 0.0 copy-done.1
  146.5 0.0 copy-done.3
  146.5 0.0 copy-done.4
  146.6 1.1 fusion.4
  (13 shorter events, 0.2 us)
Async XLA Ops:
  0.6 0.7 copy-start.5
  1.4 0.7 copy-start.6
  2.4 0.7 copy-start.7
  4.7 139.7 %copy-start = (f32[4,44,512]{2,0,1:T(4,128)S(1)}, f32[4,44,512]{2,0,1:T(4,128)}, u32[]{:S(2)}) copy-start(f32[4,44,512]{2,0,1:T(4,128)} %param.14) | copy-start | bytes 1081348
  4.7 139.8 %copy-start.2 = (bf16[4,44,512]{2,0,1:T(4,128)(2,1)S(1)}, bf16[4,44,512]{2,0,1:T(4,128)(2,1)}, u32[]{:S(2)}) copy-start(bf16[4,44,512]{2,0,1:T(4,128)(2,1)} %param.16) | copy-start | bytes 540676
  144.4 2.1 %copy-start.1 = (f32[4,44,512]{2,0,1:T(4,128)S(1)}, f32[4,44,512]{2,0,1:T(4,128)}, u32[]{:S(2)}) copy-start(f32[4,44,512]{2,0,1:T(4,128)} %param.15) | copy-start | bytes 1081348
  144.4 2.1 %copy-start.3 = (bf16[4,44,512]{2,0,1:T(4,128)(2,1)S(1)}, bf16[4,44,512]{2,0,1:T(4,128)(2,1)}, u32[]{:S(2)}) copy-start(bf16[4,44,512]{2,0,1:T(4,128)(2,1)} %param.17) | copy-start | bytes 540676
  144.4 2.1 %copy-start.4 = (bf16[44,4,512]{2,1,0:T(4,128)(2,1)S(1)}, bf16[44,4,512]{2,1,0:T(4,128)(2,1)}, u32[]{:S(2)}) copy-start(bf16[44,4,512]{2,1,0:T(4,128)(2,1)} %get-tuple-element.7) | copy-start | bytes 540676

commit v4 on v3

--- a/solution.py
+++ b/solution.py
@@ -46,17 +46,29 @@
     return (activated, slopes)
 
 
-def row_slots(lengths, targets, row_count, path_count, capacity):
-    ends = jnp.cumsum(lengths)
-    row_ids = jnp.arange(row_count, dtype=jnp.int32)
-    doc_of_row = jnp.sum((row_ids[:, None] >= ends[None, :]).astype(jnp.int32), axis=1)
-    doc_hit = doc_of_row[:, None] == jnp.arange(lengths.shape[0], dtype=jnp.int32)[None, :]
-    row_path = jnp.sum(jnp.where(doc_hit, targets[None, :], 0), axis=1)
-    path_hit = (row_path[:, None] == jnp.arange(path_count, dtype=jnp.int32)[None, :]).astype(
-        jnp.int32
+def row_slots(lengths, targets):
+    docs = lengths.shape[1]
+    before = (
+        lax.broadcasted_iota(jnp.int32, (docs, docs), 0)
+        <= lax.broadcasted_iota(jnp.int32, (docs, docs), 1)
+    ).astype(F32)
+    counts = jnp.broadcast_to(lengths, (8, docs)).astype(F32)
+    paths = jnp.broadcast_to(targets, (8, docs)).astype(F32)
+    ends = jnp.dot(counts.astype(BF), before.astype(BF), preferred_element_type=F32)[0:1, :]
+    row = lax.broadcasted_iota(jnp.int32, (192, docs), 0).astype(F32)
+    doc = lax.broadcasted_iota(jnp.int32, (192, docs), 1).astype(F32)
+    doc_of_row = jnp.sum((row >= ends).astype(F32), axis=1, keepdims=True)
+    hit = (doc_of_row == doc).astype(F32)
+    path_column = jnp.sum(hit * paths[0:1, :], axis=1, keepdims=True)
+    path_row = lax.dot_general(
+        paths.astype(BF), hit.astype(BF), (((1,), (1,)), ((), ())), preferred_element_type=F32
+    )[0:1, :]
+    earlier = lax.broadcasted_iota(jnp.int32, (192, 192), 0) < lax.broadcasted_iota(
+        jnp.int32, (192, 192), 1
     )
-    ranks = jnp.sum((jnp.cumsum(path_hit, axis=0) - 1) * path_hit, axis=1)
-    return jnp.where(ranks < capacity, row_path * capacity + ranks, -1)
+    same = jnp.where(earlier, (path_column == path_row).astype(F32), 0.0)
+    rank = jnp.sum(same, axis=0, keepdims=True)
+    return jnp.where(rank < 4.0, path_row * 4.0 + rank, -1.0)
 
 
 def outer_update(master, moment, summed, counts):
@@ -88,7 +100,8 @@
 def fused_kernel(
     tokens,
     out_grad,
-    slots_ref,
+    lengths_ref,
+    targets_ref,
     up_master,
     down_master,
     member_ref,
@@ -202,7 +215,10 @@
         low = chosen_ref[:, n * USED : (n + 1) * USED]
         high = chosen_ref[:, (n + 6) * USED : (n + 7) * USED]
         blocks_ref[:, n * BLOCK : n * BLOCK + USED] = jnp.where(y_hi == 0, low, high)
-    placing = (lax.broadcasted_iota(jnp.int32, (192, 192), 0) == slots_ref[...]).astype(F32)
+    placing = (
+        lax.broadcasted_iota(jnp.int32, (192, 192), 0).astype(F32)
+        == row_slots(lengths_ref[...], targets_ref[...])
+    ).astype(F32)
     padded[...] = jnp.dot(
         placing.astype(BF), blocks_ref[...], preferred_element_type=F32
     ).astype(BF)
@@ -537,18 +553,18 @@
     def deltas(level, offset):
         base = ((q_first + 6 + offset) % 6) * 384
         chosen = choice[level]
+        members = [member_ref[level, z * NYL + i] for i in range(4)]
 
         def body(i, carry):
             here = pl.ds(aligned(base + i * 32, 32), 32)
-            modules = [
-                weights[level][here, m * 128 : (m + 1) * 128].astype(F32) for m in range(4)
-            ]
+            modules = [weights[level][here, m * 128 : (m + 1) * 128] for m in range(4)]
             totals = [None] * 4
             for p in range(4):
                 gradient_p = grads[here, p * 128 : (p + 1) * 128]
-                weight_p = chosen[p][0] * modules[0]
+                weight_p = modules[0]
                 for m in range(1, 4):
-                    weight_p = weight_p + chosen[p][m] * modules[m]
+                    weight_p = jnp.where(members[p] == m, modules[m], weight_p)
+                weight_p = weight_p.astype(F32)
                 size = jnp.abs(gradient_p) + adam_epsilon
                 inverse = pl.reciprocal(size, approx=True)
                 inverse = inverse * (2.0 - size * inverse)
@@ -579,7 +595,7 @@
         if (level, t - 1, side, h) in rcopies:
             rcopies[level, t - 1, side, h].wait_recv()
             held = held_part(level, side, t - 1, h)
-            held[...] = (held[...].astype(F32) + src[...].astype(F32)).astype(BF)
+            held[...] = held[...] + src[...]
             src = held
         rcopies[level, t, side, h] = start(
             src, held_part(level, side, t, h), r_sem.at[level, t, side, h], to_z[side]
@@ -639,10 +655,10 @@
     b_x_got(0, 0)
     b_x_got(0, 1)
     a_x_got(2)
+    z_got(0, 1, 0, 0)
     a_y_got(1, 0, 0)
-    z_got(0, 1, 0, 0)
+    z_got(0, 1, 1, 0)
     a_y_got(1, 0, 1)
-    z_got(0, 1, 1, 0)
     a_y_got(2, 0, 0)
     a_y_got(2, 0, 1)
     b_x_got(1, 0)
@@ -651,90 +667,92 @@
     b_y_got(1, 0)
     trades.append(trade_columns(1))
     b_y_got(1, 1)
+    a_y_got(0, 1, 0)
     z_got(0, 1, 1, 1)
+    a_y_got(0, 1, 1)
     b_x_got(2, 0)
-    a_y_got(0, 1, 0)
     b_x_got(2, 1)
-    a_y_got(0, 1, 1)
     a_y_got(3, 0, 0)
     a_y_got(3, 0, 1)
-    z_got(0, 2, 0, 0)
-    f_got(0)
     a_y_got(1, 1, 0)
     a_y_got(1, 1, 1)
+    f_got(0)
+    z_got(0, 2, 0, 0)
     z_got(0, 2, 1, 0)
-    f_got(1)
     a_y_got(2, 1, 0)
     a_y_got(2, 1, 1)
+    f_got(1)
+    z_got(0, 2, 0, 1)
     b_x_got(3, 0)
-    z_got(0, 2, 0, 1)
+    b_y_got(2, 0)
     b_x_got(3, 1)
-    b_y_got(2, 0)
+    b_x_got(4, 0)
     z_got(0, 2, 1, 1)
-    b_x_got(4, 0)
     b_x_got(4, 1)
+    f_got(2)
     z_got(0, 3, 0, 0)
-    f_got(2)
+    z_first(1)
     z_got(0, 3, 1, 0)
-    f_got(3)
-    z_got(0, 3, 0, 1)
+    b_y_got(2, 1)
+    a_y_got(0, 2, 0)
     b_x_got(5, 0)
-    b_y_got(2, 1)
-    z_first(1)
-    z_got(0, 3, 1, 1)
-    a_y_got(0, 2, 0)
     a_y_got(0, 2, 1)
     b_x_got(5, 1)
     a_y_got(3, 1, 0)
+    z_got(0, 3, 0, 1)
+    a_y_got(3, 1, 1)
+    z_got(0, 3, 1, 1)
+    a_y_got(1, 2, 0)
     f_got(4)
-    a_y_got(3, 1, 1)
-    z_got(0, 4, 0, 0)
-    a_y_got(1, 2, 0)
     a_y_got(1, 2, 1)
-    z_got(0, 4, 1, 0)
+    f_got(3)
     a_y_got(2, 2, 0)
     a_y_got(2, 2, 1)
+    b_y_got(3, 0)
+    core_send(0)
+    z_got(0, 4, 0, 0)
+    a_y_got(0, 3, 0)
+    z_got(1, 0, 1, 0)
     b_x_got(6, 0)
     b_x_got(6, 1)
-    z_got(0, 4, 0, 1)
-    b_y_got(3, 0)
-    core_send(0)
-    a_y_got(0, 3, 0)
-    z_got(1, 0, 1, 0)
+    a_y_got(3, 2, 0)
+    z_got(1, 0, 0, 0)
     a_y_got(3, 2, 1)
-    f_got(5)
-    z_got(1, 0, 0, 0)
-    a_y_got(3, 2, 0)
     a_y_got(1, 3, 0)
     z_got(1, 0, 1, 1)
-    f_got(6)
+    f_got(5)
+    a_y_got(2, 3, 0)
     z_got(1, 0, 0, 1)
-    a_y_got(2, 3, 0)
     scopies[0].wait_recv()
+    b_x_got(7, 0)
+    core_send(2)
     b_x_got(7, 1)
     core_send(3)
-    b_x_got(7, 0)
-    core_send(2)
-    z_got(0, 4, 1, 1)
+    z_got(0, 4, 1, 0)
     a_y_got(3, 3, 0)
     core_send(1)
+    z_got(0, 4, 0, 1)
+    f_got(6)
+    z_got(0, 4, 1, 1)
     z_got(0, 5, 0, 0)
+    scopies[2].wait_recv()
     z_got(1, 1, 1, 0)
+    f_got(7)
+    core_send(4)
     scopies[3].wait_recv()
     z_got(1, 1, 0, 0)
-    f_got(7)
-    core_send(4)
-    scopies[2].wait_recv()
     z_got(1, 1, 1, 1)
+    scopies[1].wait_recv()
     z_got(1, 1, 0, 1)
     z_got(0, 5, 1, 1)
-    scopies[1].wait_recv()
     scopies[4].wait_recv()
-    forward(0, 2)
+    forward(0, 1)
+    forward(1, 2)
     z_got(1, 2, 0, 0)
     z_got(1, 2, 1, 0)
+    forward(2, 3)
+    forward(3, 4)
     z_got(1, 2, 0, 1)
-    forward(2, 4)
     z_got(1, 2, 1, 1)
     row_sums(0, act_ref, act_ref)
     sums_send(0, 0)
@@ -752,10 +770,13 @@
     z_got(1, 4, 0, 1)
     z_got(1, 4, 1, 1)
     make_hidden(sums_wait(0, 1))
-    gradient(1, 0, 2)
+    gradient(1, 0, 1)
+    gradient(1, 1, 2)
+    gradient(1, 2, 3)
     z_got(1, 5, 0, 0)
-    gradient(1, 2, 4)
-    gradient(1, 4, 6)
+    gradient(1, 3, 4)
+    gradient(1, 4, 5)
+    gradient(1, 5, 6)
     z_got(1, 5, 1, 1)
     deltas(1, 0)
     ring_part(1, 0, 0, 0)
@@ -764,68 +785,73 @@
     deltas(1, 1)
     ring_part(1, 1, 1, 0)
     ring_part(1, 1, 0, 1)
-    backward(0, 2)
-    backward(2, 4)
+    backward(0, 1)
+    backward(1, 2)
+    backward(2, 3)
+    backward(3, 4)
     ring_part(1, 1, 1, 1)
     ring_part(1, 1, 0, 0)
+    row_sums(1, back_ref, act_ref)
+    sums_send(1, 0)
     ring_part(1, 2, 0, 1)
     ring_part(1, 2, 1, 0)
-    row_sums(1, back_ref, act_ref)
-    sums_send(1, 0)
     deltas(1, -2)
     deltas(1, 2)
+    deltas(1, 3)
     ring_part(1, 2, 1, 1)
-    deltas(1, 3)
     ring_part(1, 2, 0, 0)
-    turn(0, 0, 6)
     mid_ref[1] = sums_wait(1, 0)
     sums_send(1, 1)
+    turn(0, 0, 6)
+    ring_part(1, 3, 0, 1)
     ring_part(1, 3, 1, 0)
-    ring_part(1, 3, 0, 1)
     turn(0, 6, 12)
+    turn(0, 12, 18)
     ring_part(1, 3, 1, 1)
-    turn(0, 12, 18)
     ring_part(1, 3, 0, 0)
     make_dpre(sums_wait(1, 1))
-    gradient(0, 0, 2)
+    gradient(0, 0, 1)
+    ring_part(1, 4, 0, 1)
+    gradient(0, 1, 2)
     ring_part(1, 4, 1, 0)
-    ring_part(1, 4, 0, 1)
+    gradient(0, 2, 3)
+    gradient(0, 3, 4)
     ring_part(1, 4, 1, 1)
-    gradient(0, 2, 4)
     ring_part(1, 4, 0, 0)
-    gradient(0, 4, 6)
+    gradient(0, 4, 5)
+    gradient(0, 5, 6)
     deltas(0, 0)
+    ring_part(1, 5, 0, 1)
     ring_part(0, 0, 0, 0)
     ring_part(0, 0, 1, 1)
+    deltas(0, -1)
     ring_part(1, 5, 1, 0)
-    ring_part(1, 5, 0, 1)
-    deltas(0, -1)
     deltas(0, 1)
-    ring_part(1, 5, 1, 1)
-    ring_part(1, 5, 0, 0)
     ring_part(0, 1, 1, 0)
     ring_part(0, 1, 0, 1)
     deltas(0, -2)
+    ring_part(1, 5, 1, 1)
+    ring_part(1, 5, 0, 0)
+    deltas(0, 2)
+    deltas(0, 3)
     ring_part(0, 1, 1, 1)
     ring_part(0, 1, 0, 0)
-    deltas(0, 2)
-    deltas(0, 3)
+    ring_part(0, 2, 0, 1)
+    ring_part(0, 2, 1, 0)
     finish(1)
-    ring_part(0, 2, 1, 0)
-    ring_part(0, 2, 0, 1)
     ring_part(0, 2, 1, 1)
     ring_part(0, 2, 0, 0)
+    ring_part(0, 3, 0, 1)
     ring_part(0, 3, 1, 0)
-    ring_part(0, 3, 0, 1)
-    outer(1)
     ring_part(0, 3, 1, 1)
     ring_part(0, 3, 0, 0)
+    outer(1)
+    ring_part(0, 4, 0, 1)
     ring_part(0, 4, 1, 0)
-    ring_part(0, 4, 0, 1)
     ring_part(0, 4, 1, 1)
     ring_part(0, 4, 0, 0)
+    ring_part(0, 5, 0, 1)
     ring_part(0, 5, 1, 0)
-    ring_part(0, 5, 0, 1)
     ring_part(0, 5, 1, 1)
     ring_part(0, 5, 0, 0)
     finish(0)
@@ -846,13 +872,13 @@
 DMA = pltpu.SemaphoreType.DMA
 
 
-def fused(tokens, out_grad, slots, masters, members):
+def fused(tokens, out_grad, lengths, targets, masters, members):
     shape = masters[0].shape
     sums = jax.ShapeDtypeStruct(shape, BF)
     return pl.pallas_call(
         fused_kernel,
         out_shape=(sums, sums),
-        in_specs=[VMEM, VMEM, VMEM, VMEM, VMEM, SMEM],
+        in_specs=[VMEM, VMEM, VMEM, VMEM, VMEM, VMEM, SMEM],
         out_specs=(VMEM, VMEM),
         scratch_shapes=[
             pltpu.VMEM((2, 16, 512), F32),
@@ -900,7 +926,7 @@
             collective_id=0, has_side_effects=True, vmem_limit_bytes=56 * 1024 * 1024
         ),
         name="fused",
-    )(tokens, out_grad, slots, *masters, members)
+    )(tokens, out_grad, lengths, targets, *masters, members)
 
 
 def on_device(
@@ -914,17 +940,16 @@
     up_moment,
     down_moment,
 ):
-    path_count = lax.axis_size("path")
-    row_count = tokens.shape[0]
-    capacity = row_count // path_count
-
-    slots = row_slots(doc_lengths[0], doc_paths[0], row_count, path_count, capacity)
-
     def turned(array):
         return array.transpose(1, 0, 2)
 
     sums = fused(
-        tokens, out_grad, slots[None, :], (turned(up_master), turned(down_master)), membership.T
+        tokens,
+        out_grad,
+        doc_lengths,
+        doc_paths,
+        (turned(up_master), turned(down_master)),
+        membership.T,
     )
     module_ids = jnp.arange(up_master.shape[0], dtype=jnp.int32)
 

time: 148 us -> 143 us (0.966)
  Pallas kernels: 140 us -> 137 us
  other arithmetic: 5.01 us -> 3.32 us
    pallas_call x1, Pallas kernels: 140 us -> 137 us  [fused(): pl.pallas_call(fused_kernel, out_shape=(sums, sums), in_specs=[VMEM, VMEM...]
where the time goes in v4:
time: 143 us; the launch traced here: 142 us
  Pallas kernels  137 us (96%)
  other arithmetic  3.32 us (2%)
    pallas_call x1, Pallas kernels, fused(): pl.pallas_call(fused_kernel, out_shape=(sums, sums), in_specs=[VMEM, VMEM...  137 us
    convert_element_type x2, other arithmetic, outer_update(): buffer.astype(jnp.bfloat16)  3.2 us

profile of v4, /device:TPU:56, one launch (start us, length us, event | category | flops | bytes accessed | tf_op | source)
XLA Modules:
  0.0 142.2 jit_solution(8373032385824169551)
XLA Ops:
  0.6 0.0 copy-start.5
  0.6 0.7 copy-done.5
  1.3 0.1 convert_reduce_fusion
  1.5 0.0 copy-start
  1.5 0.0 copy-start.2
  1.5 137.5 %fused.1 = (bf16[44,4,512]{2,1,0:T(4,128)(2,1)}, bf16[44,4,512]{2,1,0:T(4,128)(2,1)}) custom-call(bf16[192,2112]{1,0:T(8,128)(2,1)} %tokens.1, bf16[192,2112]{1,0:T(8,128)(2,1)} %out_grad.1, s32[1,24]{1,0:T(1,128)} %lengths_ref.1, s32[1,24]{1,0:T(1,128)} %targets_ref.1, f32[44,4,512]{2,1,0:T(4,128)} %bitcast.29, f32[44,4,512]{2,1,0:T(4,128)} %bitcast.30, ...), custom_call_target="tpu_custom_call" | custom-call | tf_op jit(solution)/shard_map/fused/pallas_call | solution.py:878
  139.0 0.0 copy-done
  139.0 0.0 copy-done.2
  139.0 0.0 copy-start.1
  139.0 0.0 copy-start.3
  139.0 0.0 copy-start.4
  139.0 2.1 %fusion.5 = (bf16[4,44,512]{2,0,1:T(4,128)(2,1)}, f32[4,44,512]{2,0,1:T(4,128)}) fusion(bf16[4,44,512]{2,0,1:T(4,128)(2,1)S(1)} %copy-done.2, f32[4]{0:T(128)S(1)} %broadcast_maximum_fusion.1, bf16[44,4,512]{2,1,0:T(4,128)(2,1)} %get-tuple-element.6, f32[4,44,512]{2,0,1:T(4,128)S(1)} %copy-done), kind=kLoop, calls=%fused_computation.10 | loop fusion | flops 991232 | bytes 1261584 | tf_op jit(solution)/shard_map/convert_element_type | solution.py:77
  141.1 0.0 copy-done.1
  141.1 0.0 copy-done.3
  141.1 0.0 copy-done.4
  141.1 1.1 fusion.4
  (3 shorter events, 0.0 us)
Async XLA Ops:
  0.6 0.7 copy-start.5
  1.5 137.5 %copy-start = (f32[4,44,512]{2,0,1:T(4,128)S(1)}, f32[4,44,512]{2,0,1:T(4,128)}, u32[]{:S(2)}) copy-start(f32[4,44,512]{2,0,1:T(4,128)} %param.14) | copy-start | bytes 1081348
  1.5 137.5 %copy-start.2 = (bf16[4,44,512]{2,0,1:T(4,128)(2,1)S(1)}, bf16[4,44,512]{2,0,1:T(4,128)(2,1)}, u32[]{:S(2)}) copy-start(bf16[4,44,512]{2,0,1:T(4,128)(2,1)} %param.16) | copy-start | bytes 540676
  139.0 2.1 %copy-start.1 = (f32[4,44,512]{2,0,1:T(4,128)S(1)}, f32[4,44,512]{2,0,1:T(4,128)}, u32[]{:S(2)}) copy-start(f32[4,44,512]{2,0,1:T(4,128)} %param.15) | copy-start | bytes 1081348
  139.0 2.1 %copy-start.3 = (bf16[4,44,512]{2,0,1:T(4,128)(2,1)S(1)}, bf16[4,44,512]{2,0,1:T(4,128)(2,1)}, u32[]{:S(2)}) copy-start(bf16[4,44,512]{2,0,1:T(4,128)(2,1)} %param.17) | copy-start | bytes 540676
  139.0 2.1 %copy-start.4 = (bf16[44,4,512]{2,1,0:T(4,128)(2,1)S(1)}, bf16[44,4,512]{2,1,0:T(4,128)(2,1)}, u32[]{:S(2)}) copy-start(bf16[44,4,512]{2,1,0:T(4,128)(2,1)} %get-tuple-element.7) | copy-start | bytes 540676
